TPU v7x, 1024 devices: a whole 4x4x32 slice. The times are simulated.
1024 devices in a mesh: dp: 16 (over y, x), expert: 64 (over z, core).
Axes of the slice: x: 4, y: 4, z: 32, core: 2. Of those that a mesh axis runs over, the one named last changes fastest.
Arguments:
- latent: bfloat16 [131072, 1024], P(('dp', 'expert')), may hold values from -6 to 6
- cotangent: bfloat16 [131072, 1024], P(('dp', 'expert')), may hold values from -0.59765625 to 0.59765625
- routes: int32 [131072, 1], P(('dp', 'expert')), may hold values from 0 to 63; in each aligned block of 128 rows (0 to 127, 128 to 255, ...) at most 4 rows name the same one
- gates: float32 [131072, 1], P(('dp', 'expert')), may hold values from 0.1 to 1
- w_in: bfloat16 [64, 1024, 2048], P('expert'), may hold values from -0.1875 to 0.1875
- w_out: bfloat16 [64, 1024, 1024], P('expert'), may hold values from -0.1875 to 0.1875
Outputs:
- output: bfloat16 [131072, 1024], P(('dp', 'expert'))
- grad_in: float32 [64, 1024, 2048], P('expert', 'dp')
- grad_out: float32 [64, 1024, 1024], P('expert', 'dp')
Inputs may be any that keep to these rules, and one draw needn't show every extreme that they name: In each aligned block of 128 tokens no expert is named by more than 4 routes, a bound that some block reaches.
All inputs are finite; a program needn't handle non-finite values.
Results may differ from a plain program's by a relative error of at most 0.018.
Values may be sent and summed in bfloat16 or wider, within the bound.
No kernel may reach another device: no remote copies, remote signals or barrier semaphores. Data moves between devices by JAX's collectives and lax.ppermute only.
A program may use at most 64 MiB of HBM per device.

v0:
```python
import jax
import jax.numpy as jnp
from jax import lax
from jax.sharding import PartitionSpec as P


def on_device(latent, cotangent, routes, gates, w_in, w_out):
    n_experts = lax.axis_size("expert")
    n_replicas = lax.axis_size("dp")
    tok_count = latent.shape[0]
    top_count = routes.shape[1]
    width = latent.shape[1]
    hidden_units = w_out.shape[2]
    capacity = max(2, 2 * tok_count * top_count // n_experts)
    route_flat = routes.reshape(-1)
    gate_flat = gates.reshape(-1)
    onehot = (route_flat[:, None] == jnp.arange(n_experts, dtype=jnp.int32)[None, :]).astype(
        jnp.int32
    )
    before = jnp.cumsum(onehot, axis=0) - onehot
    slot = jnp.sum(before * onehot, axis=1)
    position = route_flat * capacity + slot
    placing = (
        jnp.arange(n_experts * capacity, dtype=jnp.int32)[:, None] == position[None, :]
    ).astype(jnp.bfloat16)
    x_rows = jnp.repeat(latent, top_count, axis=0)
    dy_rows = (
        gate_flat[:, None] * jnp.repeat(cotangent, top_count, axis=0).astype(jnp.float32)
    ).astype(jnp.bfloat16)
    send_x = (
        jnp.dot(placing, x_rows, preferred_element_type=jnp.float32)
        .astype(jnp.bfloat16)
        .reshape(n_experts, capacity, width)
    )
    send_dy = (
        jnp.dot(placing, dy_rows, preferred_element_type=jnp.float32)
        .astype(jnp.bfloat16)
        .reshape(n_experts, capacity, width)
    )
    got_x = lax.all_to_all(send_x, "expert", split_axis=0, concat_axis=0, tiled=True)
    got_dy = None
    x_buf = got_x.reshape(-1, width)
    acts = jnp.dot(x_buf, w_in[0], preferred_element_type=jnp.float32)
    gate = acts[:, :hidden_units]
    upper = acts[:, hidden_units:]
    sig = jax.nn.sigmoid(gate)
    swish = gate * sig
    hidden = (swish * upper).astype(jnp.bfloat16)
    y_buf = lax.dot_general(
        hidden, w_out[0], (((1,), (1,)), ((), ())), preferred_element_type=jnp.float32
    ).astype(jnp.bfloat16)
    back = lax.all_to_all(
        y_buf.reshape(n_experts, capacity, width), "expert", split_axis=0, concat_axis=0, tiled=True
    ).reshape(-1, width)
    y_rows = lax.dot_general(
        placing, back, (((0,), (0,)), ((), ())), preferred_element_type=jnp.float32
    )
    output = jnp.sum(
        (gate_flat[:, None] * y_rows).reshape(tok_count, top_count, width), axis=1
    ).astype(jnp.bfloat16)
    got_dy = lax.all_to_all(send_dy, "expert", split_axis=0, concat_axis=0, tiled=True)
    dy_buf = got_dy.reshape(-1, width)
    d_hidden = jnp.dot(dy_buf, w_out[0], preferred_element_type=jnp.float32)
    d_gate = d_hidden * upper * sig * (1.0 + gate * (1.0 - sig))
    d_upper = d_hidden * swish
    d_acts = jnp.concatenate([d_gate, d_upper], axis=1).astype(jnp.bfloat16)
    share = width // n_replicas
    columns = x_buf
    grad_in = lax.psum_scatter(
        lax.dot_general(
            columns, d_acts, (((0,), (0,)), ((), ())), preferred_element_type=jnp.float32
        ).astype(jnp.bfloat16),
        "dp",
        scatter_dimension=0,
        tiled=True,
    ).astype(jnp.float32)
    columns = dy_buf
    grad_out = lax.psum_scatter(
        lax.dot_general(
            columns, hidden, (((0,), (0,)), ((), ())), preferred_element_type=jnp.float32
        ).astype(jnp.bfloat16),
        "dp",
        scatter_dimension=0,
        tiled=True,
    ).astype(jnp.float32)
    return (
        output,
        grad_in.reshape(1, share, 2 * hidden_units),
        grad_out.reshape(1, share, hidden_units),
    )


def solution(mesh):
    in_specs = (
        P(("dp", "expert"), None),
        P(("dp", "expert"), None),
        P(("dp", "expert"), None),
        P(("dp", "expert"), None),
        P("expert", None, None),
        P("expert", None, None),
    )
    out_specs = (P(("dp", "expert"), None), P("expert", "dp", None), P("expert", "dp", None))
    return jax.shard_map(
        on_device, mesh=mesh, in_specs=in_specs, out_specs=out_specs, check_vma=False
    )
```

profile of v0, /device:TPU:6, one launch (start us, length us, event | category | flops | bytes accessed | tf_op | source)
XLA Modules:
  0.0 404.9 jit_solution(12712848088119525772)
XLA Ops:
  7.2 0.0 copy-start
  7.2 0.0 copy-start.5
  7.2 0.0 copy-start.4
  7.2 0.9 fusion.18
  8.1 0.2 reduce_window_sum.11
  8.3 0.8 select_reduce_fusion
  9.1 0.7 multiply_add_fusion
  9.8 1.2 convolution_convert_fusion.3
  11.0 1.0 reshape.51
  12.0 29.3 %all-to-all-start = ((bf16[64,4,1024]{2,1,0:T(4,128)(2,1)}), bf16[64,4,1024]{2,1,0:T(4,128)(2,1)S(1)}, u32[]{:S(2)}, u32[]{:S(2)}) async-start(bf16[64,4,1024]{2,1,0:T(4,128)(2,1)} %reshape.51), calls=%async_computation | async-start | bytes 1048576 | tf_op jit(solution)/shard_map/all_to_all | solution.py:40
  41.4 0.0 copy-done.5
  41.4 0.0 copy-done.4
  41.4 0.4 convolution_convert_fusion.2
  41.8 1.0 reshape.55
  42.8 64.4 %all-to-all-done = bf16[64,4,1024]{2,1,0:T(4,128)(2,1)S(1)} async-done(((bf16[64,4,1024]{2,1,0:T(4,128)(2,1)}), bf16[64,4,1024]{2,1,0:T(4,128)(2,1)S(1)}, u32[]{:S(2)}, u32[]{:S(2)}) %all-to-all-start) | async-done | bytes 524320 | tf_op jit(solution)/shard_map/all_to_all | solution.py:40
  107.1 5.5 %all-to-all-start.2 = ((bf16[64,4,1024]{2,1,0:T(4,128)(2,1)}), bf16[64,4,1024]{2,1,0:T(4,128)(2,1)}, u32[]{:S(2)}, u32[]{:S(2)}) async-start(bf16[64,4,1024]{2,1,0:T(4,128)(2,1)} %reshape.55), calls=%async_computation.2 | async-start | bytes 1048576 | tf_op jit(solution)/shard_map/all_to_all | solution.py:61
  112.6 0.0 reduce-scatter.5.cloned.1.call-start
  112.7 0.1 reshape.52
  112.8 4.8 %fusion = f32[256,2048]{1,0:T(8,128)} fusion(bf16[256,1024]{1,0:T(8,128)(2,1)S(1)} %reshape.52, bf16[1,1024,2048]{2,1,0:T(8,128)(2,1)} %param.10), kind=kOutput, calls=%fused_computation | convolution fusion | flops 1073741824 | bytes 6815744 | tf_op jit(solution)/shard_map/dot_general | solution.py:43
  117.6 59.7 %all-to-all-done.2 = bf16[64,4,1024]{2,1,0:T(4,128)(2,1)} async-done(((bf16[64,4,1024]{2,1,0:T(4,128)(2,1)}), bf16[64,4,1024]{2,1,0:T(4,128)(2,1)}, u32[]{:S(2)}, u32[]{:S(2)}) %all-to-all-start.2) | async-done | bytes 524320 | tf_op jit(solution)/shard_map/all_to_all | solution.py:61
  177.2 1.2 reshape.56
  178.4 0.0 copy-done
  178.4 3.6 multiply_convert_fusion.1
  182.0 0.0 copy-start.1
  182.0 0.8 copy-done.1
  182.8 2.1 convolution_convert_fusion.1
  184.9 0.0 copy-start.3
  184.9 0.0 reduce-scatter.5.cloned.1.call-update
  184.9 0.0 reduce-scatter.3.cloned.1.call-start
  184.9 1.0 copy-done.3
  185.9 4.3 %convolution_convert_fusion = bf16[1024,2048]{1,0:T(8,128)(2,1)} fusion(bf16[256,1024]{1,0:T(8,128)(2,1)S(1)} %reshape.52, bf16[256,1024]{1,0:T(8,128)(2,1)} %get-tuple-element.4, bf16[256,1024]{1,0:T(8,128)(2,1)S(1)} %copy-done.3), kind=kOutput, calls=%fused_computation.2 | convolution fusion | flops 1077936128 | bytes 5767168 | tf_op jit(solution)/shard_map/dot_general | solution.py:70
  190.2 0.0 copy-start.2
  190.2 0.0 reduce-scatter.3.cloned.1.call-update
  190.2 1.0 copy-done.2
  191.2 0.7 fusion.6
  192.0 0.2 reshape.53
  192.2 68.6 %all_to_all.15 = bf16[64,4,1024]{2,1,0:T(4,128)(2,1)S(1)} all-to-all(bf16[64,4,1024]{2,1,0:T(4,128)(2,1)S(1)} %reshape.53), channel_id=1, replica_groups=mesh['dp'=16,'expert'=64] {'expert'}, dimensions={0} | all-to-all | bytes 1048576 | tf_op jit(solution)/shard_map/all_to_all | solution.py:52
  260.8 0.1 reshape.54
  260.9 1.0 fusion.9
  261.9 15.2 %reduce-scatter.5.cloned.1.call-done = bf16[64,1024]{1,0:T(8,128)(2,1)} async-done(((bf16[1024,1024]{1,0:T(8,128)(2,1)}), bf16[64,1024]{1,0:T(8,128)(2,1)}) %reduce-scatter.5.cloned.1.call-update) | async-done | bytes 131088 | tf_op jit(solution)/shard_map/reduce_scatter | solution.py:78
  277.1 1.6 bitcast_convert_fusion.1
  278.7 117.6 %reduce-scatter.3.cloned.1.call-done = bf16[64,2048]{1,0:T(8,128)(2,1)} async-done(((bf16[1024,2048]{1,0:T(8,128)(2,1)}), bf16[64,2048]{1,0:T(8,128)(2,1)}) %reduce-scatter.3.cloned.1.call-update) | async-done | bytes 262160 | tf_op jit(solution)/shard_map/reduce_scatter | solution.py:69
  396.3 1.8 bitcast_convert_fusion
Async XLA Ops:
  7.2 171.2 %copy-start = (bf16[1,1024,1024]{2,1,0:T(8,128)(2,1)S(1)}, bf16[1,1024,1024]{2,1,0:T(8,128)(2,1)}, u32[]{:S(2)}) copy-start(bf16[1,1024,1024]{2,1,0:T(8,128)(2,1)} %param.11) | copy-start | bytes 6291460
  7.2 34.2 %copy-start.5 = (f32[128,1]{0,1:T(1,128)S(1)}, f32[128,1]{0,1:T(1,128)}, u32[]{:S(2)}) copy-start(f32[128,1]{0,1:T(1,128)} %param.9) | copy-start | bytes 1540
  7.2 34.2 %copy-start.4 = (bf16[128,1024]{1,0:T(8,128)(2,1)S(1)}, bf16[128,1024]{1,0:T(8,128)(2,1)}, u32[]{:S(2)}) copy-start(bf16[128,1024]{1,0:T(8,128)(2,1)} %param.7) | copy-start | bytes 786436
  12.0 95.1 %all-to-all-start = ((bf16[64,4,1024]{2,1,0:T(4,128)(2,1)}), bf16[64,4,1024]{2,1,0:T(4,128)(2,1)S(1)}, u32[]{:S(2)}, u32[]{:S(2)}) async-start(bf16[64,4,1024]{2,1,0:T(4,128)(2,1)} %reshape.51), calls=%async_computation | async-start | bytes 1048576 | tf_op jit(solution)/shard_map/all_to_all | solution.py:40
  107.1 70.1 %all-to-all-start.2 = ((bf16[64,4,1024]{2,1,0:T(4,128)(2,1)}), bf16[64,4,1024]{2,1,0:T(4,128)(2,1)}, u32[]{:S(2)}, u32[]{:S(2)}) async-start(bf16[64,4,1024]{2,1,0:T(4,128)(2,1)} %reshape.55), calls=%async_computation.2 | async-start | bytes 1048576 | tf_op jit(solution)/shard_map/all_to_all | solution.py:61
  112.6 164.5 %reduce-scatter.5.cloned.1.call-start = ((), (), s32[]{:S(2)}) async-start(), calls=%async_computation.6 | async-start | bytes 2228224 | tf_op jit(solution)/shard_map/reduce_scatter | solution.py:78
  182.0 0.8 copy-start.1
  184.9 1.0 copy-start.3
  184.9 211.4 %reduce-scatter.3.cloned.1.call-start = ((), (), s32[]{:S(2)}) async-start(), calls=%async_computation.5 | async-start | bytes 4456448 | tf_op jit(solution)/shard_map/reduce_scatter | solution.py:69
  190.2 1.0 copy-start.2
Sparse Core Ops, SparseCore 0:
  185.0 92.0 reduce-scatter.4
  283.3 112.8 reduce-scatter.2
where the time goes:
time: 406 us; the launch traced here: 405 us
  waiting for transfers between devices  257 us (63%)
  blocking collectives  68.6 us (17%)
  starting transfers between devices  34.9 us (9%)
  matrix products  18 us (4%)
  between operations  14.2 us (3%)
  local copies, waits for them, and re-layouts  6.38 us (2%)
  other arithmetic  5.95 us (1%)
    reduce_scatter x1, waiting for transfers between devices, on_device(): lax.psum_scatter(lax.dot_general(columns, d_acts, (((0,), (0,)), ((), ())...  118 us
    all_to_all x1, blocking collectives, on_device(): lax.all_to_all(y_buf.reshape(n_experts, capacity, width), 'expert', split...  68.6 us
    all_to_all x1, waiting for transfers between devices, on_device(): lax.all_to_all(send_x, 'expert', split_axis=0, concat_axis=0, tiled=True)  64.4 us
    all_to_all x1, waiting for transfers between devices, on_device(): lax.all_to_all(send_dy, 'expert', split_axis=0, concat_axis=0, tiled=True)  59.7 us
    all_to_all x1, starting transfers between devices, on_device(): lax.all_to_all(send_x, 'expert', split_axis=0, concat_axis=0, tiled=True)  29.3 us
    reduce_scatter x1, waiting for transfers between devices, on_device(): lax.psum_scatter(lax.dot_general(columns, hidden, (((0,), (0,)), ((), ())...  15.2 us
  transfers between devices with their start and end apart: 4, of which 4 were waited for; matrix products, arithmetic and copies ran while one was open for 4% of the time, Pallas kernels for 0%

commit v1 on v0

v1 whole, which is shorter than its diff:
```python
import functools
import jax
import jax.numpy as jnp
from jax import lax
from jax.experimental import pallas as pl
from jax.experimental.pallas import tpu as pltpu
from jax.sharding import PartitionSpec as P

BF = jnp.bfloat16
F32 = jnp.float32
MIB = 1 << 20
RING = 4


def call(body, outs, flops, moved, n_in, scalars=0, vmem=32, scratch=()):
    vm = pl.BlockSpec(memory_space=pltpu.VMEM)
    sm = pl.BlockSpec(memory_space=pltpu.SMEM)
    return pl.pallas_call(
        body,
        out_shape=[jax.ShapeDtypeStruct(s, t) for s, t in outs],
        in_specs=[sm] * scalars + [vm] * n_in,
        out_specs=[vm] * len(outs),
        scratch_shapes=list(scratch),
        compiler_params=pltpu.CompilerParams(vmem_limit_bytes=vmem * MIB),
        cost_estimate=pl.CostEstimate(flops=flops, bytes_accessed=moved, transcendentals=0),
    )


def dot(a, b, dims):
    return lax.dot_general(a, b, (dims, ((), ())), preferred_element_type=F32)


def place_kernel(cap, x_ref, c_ref, r_ref, g_ref, send_ref, pos_ref):
    tok = x_ref.shape[0]
    r = jnp.broadcast_to(r_ref[...], (tok, tok))
    g = jnp.transpose(jnp.broadcast_to(g_ref[...], (tok, tok)))[:, :1]
    row = lax.broadcasted_iota(jnp.int32, (tok, tok), 0)
    col = lax.broadcasted_iota(jnp.int32, (tok, tok), 1)
    same = jnp.where((jnp.transpose(r) == r) & (row < col), 1, 0)
    slot = jnp.sum(same, axis=0, keepdims=True)
    route = r_ref[...]
    pos_ref[...] = route * cap + slot
    at = route * (2 * cap) + slot
    at = jnp.concatenate([at, at + cap], axis=1)
    rows = lax.broadcasted_iota(jnp.int32, (send_ref.shape[0], 2 * tok), 0)
    placing = jnp.where(rows == at, 1.0, 0.0).astype(BF)
    dy = (g * c_ref[...].astype(F32)).astype(BF)
    both = jnp.concatenate([x_ref[...], dy], axis=0)
    send_ref[...] = dot(placing, both, ((1,), (0,))).astype(BF)


def forward_kernel(cap, got_ref, wi_ref, wo_ref, y_ref, x_ref, dy_ref, hid_ref, gu_ref):
    n = x_ref.shape[0]
    hidden = wo_ref.shape[1]
    r = lax.broadcasted_iota(jnp.int32, (n, 2 * n), 0)
    c = lax.broadcasted_iota(jnp.int32, (n, 2 * n), 1)
    at = (r // cap) * (2 * cap) + r % cap
    got = got_ref[...]
    x = dot(jnp.where(c == at, 1.0, 0.0).astype(BF), got, ((1,), (0,))).astype(BF)
    x_ref[...] = x
    step = 512
    for h in range(0, hidden, step):
        g = dot(x, wi_ref[:, h : h + step], ((1,), (0,)))
        u = dot(x, wi_ref[:, hidden + h : hidden + h + step], ((1,), (0,)))
        gu_ref[:, h : h + step] = g
        gu_ref[:, hidden + h : hidden + h + step] = u
        hid_ref[:, h : h + step] = (g * jax.nn.sigmoid(g) * u).astype(BF)
    y_ref[...] = dot(hid_ref[...], wo_ref[...], ((1,), (1,))).astype(BF)
    dy_ref[...] = dot(jnp.where(c == at + cap, 1.0, 0.0).astype(BF), got, ((1,), (0,))).astype(BF)


def backward_kernel(me_ref, x_ref, dy_ref, hid_ref, gu_ref, wo_ref, *refs):
    a, b = refs[:RING], refs[RING : 2 * RING]
    da_ref, acc_ref = refs[2 * RING :]
    n, hidden = hid_ref.shape
    dy = dy_ref[...]
    step = 512
    for h in range(0, hidden, step):
        dh = dot(dy, wo_ref[:, h : h + step], ((1,), (0,)))
        g = gu_ref[:, h : h + step]
        u = gu_ref[:, hidden + h : hidden + h + step]
        sig = jax.nn.sigmoid(g)
        da_ref[:, h : h + step] = (dh * u * sig * (1.0 + g * (1.0 - sig))).astype(BF)
        da_ref[:, hidden + h : hidden + h + step] = (dh * (g * sig)).astype(BF)
    me_y, me_x = me_ref[0], me_ref[1]
    block = x_ref.shape[1] // RING
    share = block // RING
    half_in, half_out = hidden, hidden // 2

    def half(k, lhs_x, lhs_dy):
        acc_ref[:, :half_in] = dot(lhs_x, da_ref[:, k * half_in : (k + 1) * half_in], ((0,), (0,))).astype(BF)
        acc_ref[:, half_in:] = dot(lhs_dy, hid_ref[:, k * half_out : (k + 1) * half_out], ((0,), (0,))).astype(BF)

    for y in range(RING):
        cols = slice(y * block, (y + 1) * block)
        half(0, x_ref[:, cols], dy_ref[:, cols])
        for s in range(RING):
            at = pl.multiple_of(((me_x + s) % RING) * share, share)
            a[s][y] = acc_ref[pl.ds(at, share), :]
    for s in range(RING):
        at = pl.multiple_of(((me_y + s) % RING) * block, block)
        half(1, x_ref[:, pl.ds(at, block)], dy_ref[:, pl.ds(at, block)])
        for x in range(RING):
            b[s][x] = acc_ref[x * share : (x + 1) * share, :]


def middle_kernel(me_ref, *refs):
    a, b = refs[:RING], refs[RING : 2 * RING]
    a_out, b_out = refs[2 * RING : 3 * RING], refs[3 * RING :]
    for parts, outs, me in ((a, a_out, me_ref[0]), (b, b_out, me_ref[1])):
        for t in range(RING):
            at = (me + t) % RING
            total = parts[0][at].astype(F32)
            for part in parts[1:]:
                total = total + part[at].astype(F32)
            outs[t][...] = total.astype(outs[t].dtype)


def last_kernel(*refs):
    a, b = refs[:RING], refs[RING : 2 * RING]
    in_ref, out_ref = refs[2 * RING :]
    half_in, half_out = in_ref.shape[1] // 2, out_ref.shape[1] // 2
    for k, parts in enumerate((a, b)):
        total = parts[0][...]
        for part in parts[1:]:
            total = total + part[...].astype(F32)
        in_ref[:, k * half_in : (k + 1) * half_in] = total[:, :half_in]
        out_ref[:, k * half_out : (k + 1) * half_out] = total[:, half_in:]


def on_device(latent, cotangent, routes, gates, w_in, w_out):
    n_experts = lax.axis_size("expert")
    tok, width = latent.shape
    hidden = w_out.shape[2]
    cap = max(2, 2 * tok // n_experts)
    rows = n_experts * cap
    me = lax.axis_index("dp")
    me = jnp.stack([me // RING, me % RING]).astype(jnp.int32)
    gate_row = gates.reshape(1, tok)

    send, pos = call(
        functools.partial(place_kernel, cap),
        [((2 * rows, width), BF), ((1, tok), jnp.int32)],
        4 * rows * tok * width * 2, 4 * MIB, 4,
    )(latent, cotangent, routes.reshape(1, tok), gate_row)
    got = lax.all_to_all(
        send.reshape(n_experts, 2 * cap, width), "expert", split_axis=0, concat_axis=0, tiled=True
    ).reshape(2 * rows, width)

    y_buf, x_buf, dy_buf, hid, gu = call(
        functools.partial(forward_kernel, cap),
        [
            ((rows, width), BF),
            ((rows, width), BF),
            ((rows, width), BF),
            ((rows, hidden), BF),
            ((rows, 2 * hidden), F32),
        ],
        2 * rows * width * hidden * 5, 12 * MIB, 3, vmem=40,
    )(got, w_in[0], w_out[0])
    back = lax.all_to_all(
        y_buf.reshape(n_experts, cap, width), "expert", split_axis=0, concat_axis=0, tiled=True
    ).reshape(rows, width)

    share = width // (RING * RING)
    cols = hidden + hidden // 2
    parts = call(
        backward_kernel,
        [((RING, share, cols), BF)] * (2 * RING),
        2 * rows * width * hidden * 4, 16 * MIB, 5, scalars=1, vmem=40,
        scratch=[pltpu.VMEM((rows, 2 * hidden), BF), pltpu.VMEM((width // RING, cols), BF)],
    )(me, x_buf, dy_buf, hid, gu, w_out[0])

    ring = range(RING)

    def along_x(v, s):
        return lax.ppermute(v, "dp", [(RING * y + x, RING * y + (x + s) % RING) for y in ring for x in ring])

    def along_y(v, s):
        return lax.ppermute(v, "dp", [(RING * y + x, RING * ((y + s) % RING) + x) for y in ring for x in ring])

    a, b = parts[:RING], parts[RING:]
    a = [a[0]] + [along_x(a[s], s) for s in (1, 2, 3)]
    b = [b[0]] + [along_y(b[s], s) for s in (1, 2, 3)]
    mids = call(
        middle_kernel,
        ([((share, cols), F32)] + [((share, cols), BF)] * (RING - 1)) * 2,
        16 * MIB, 10 * MIB, 2 * RING, scalars=1,
    )(me, *a, *b)
    a, b = mids[:RING], mids[RING:]
    a = [a[0]] + [along_y(a[s], s) for s in (1, 2, 3)]
    b = [b[0]] + [along_x(b[s], s) for s in (1, 2, 3)]
    grad_in, grad_out = call(
        last_kernel,
        [((share, 2 * hidden), F32), ((share, hidden), F32)],
        4 * MIB, 4 * MIB, 2 * RING,
    )(*a, *b)

    placing = (jnp.arange(rows, dtype=jnp.int32)[:, None] == pos).astype(BF)
    y_rows = dot(placing, back, ((0,), (0,)))
    output = (gates * y_rows).astype(BF)
    return output, grad_in[None], grad_out[None]


def solution(mesh):
    tokens = P(("dp", "expert"), None)
    return jax.shard_map(
        on_device,
        mesh=mesh,
        in_specs=(tokens,) * 4 + (P("expert", None, None),) * 2,
        out_specs=(tokens, P("expert", "dp", None), P("expert", "dp", None)),
        check_vma=False,
    )
```

time: 406 us -> 250 us (0.62)
  waiting for transfers between devices: 257 us -> 35.8 us
  blocking collectives: 68.6 us -> 140 us
  matrix products: 18 us -> 0.98 us
  starting transfers between devices: 34.9 us -> 49 us
  between operations: 14.2 us -> 0.87 us
  Pallas kernels: 0 us -> 8.85 us
  local copies, waits for them, and re-layouts: 6.38 us -> 14.2 us
  other arithmetic: 5.95 us -> 0.08 us
    reduce_scatter x2 -> x0, waiting for transfers between devices: 133 us -> none  [the longest x1 118 us: on_device(): lax.psum_scatter(lax.dot_general(columns, d_acts, (((0,), (0,)), ((), ())...]
    all_to_all x2 -> x1, waiting for transfers between devices: 124 us -> 0.01 us  [on_device(): lax.all_to_all(y_buf.reshape(n_experts, cap, width), 'expert', split_axis...]
    all_to_all x1, blocking collectives: 68.6 us -> 140 us  [on_device(): lax.all_to_all(send.reshape(n_experts, 2 * cap, width), 'expert', split_a...]
    ppermute x0 -> x12, starting transfers between devices: none -> 43.5 us  [the longest x6 24.7 us: along_y(): lax.ppermute(v, 'dp', [(RING * y + x, RING * ((y + s) % RING) + x) for y...]
    ppermute x0 -> x12, waiting for transfers between devices: none -> 35.8 us  [the longest x6 27.5 us: along_x(): lax.ppermute(v, 'dp', [(RING * y + x, RING * y + (x + s) % RING) for y in...]
    all_to_all x2 -> x1, starting transfers between devices: 34.8 us -> 5.49 us  [on_device(): lax.all_to_all(y_buf.reshape(n_experts, cap, width), 'expert', split_axis...]
    dot_general x8 -> x1, matrix products: 18 us -> 0.98 us  [dot(): return lax.dot_general(a, b, (dims, ((), ())), preferred_element_type=F32)]
    unnamed x12 -> x26, local copies, waits for them, and re-layouts: 2.8 us -> 12 us
  transfers between devices with their start and end apart: 4 -> 13, of which waited for: 4 -> 7; matrix products, arithmetic and copies ran while one was open for 4% -> 0% of each run, Pallas kernels for 0% -> 2%
where the time goes in v1:
time: 250 us
  blocking collectives  140 us (56%)
  starting transfers between devices  49 us (20%)
  waiting for transfers between devices  35.8 us (14%)
  local copies, waits for them, and re-layouts  14.2 us (6%)
  Pallas kernels  8.85 us (4%)
    all_to_all x1, blocking collectives, on_device(): lax.all_to_all(send.reshape(n_experts, 2 * cap, width), 'expert', split_a...  140 us
    ppermute x6, waiting for transfers between devices, along_x(): lax.ppermute(v, 'dp', [(RING * y + x, RING * y + (x + s) % RING) for y in...  27.5 us
    ppermute x6, starting transfers between devices, along_y(): lax.ppermute(v, 'dp', [(RING * y + x, RING * ((y + s) % RING) + x) for y...  24.7 us
    ppermute x6, starting transfers between devices, along_x(): lax.ppermute(v, 'dp', [(RING * y + x, RING * y + (x + s) % RING) for y in...  18.8 us
    unnamed x26, local copies, waits for them, and re-layouts  12 us
    ppermute x6, waiting for transfers between devices, along_y(): lax.ppermute(v, 'dp', [(RING * y + x, RING * ((y + s) % RING) + x) for y...  8.28 us
    all_to_all x1, starting transfers between devices, on_device(): lax.all_to_all(y_buf.reshape(n_experts, cap, width), 'expert', split_axis...  5.49 us
  transfers between devices with their start and end apart: 13, of which 7 were waited for; matrix products, arithmetic and copies ran while one was open for 0% of the time, Pallas kernels for 2%

profile of v1, /device:TPU:6, one launch (start us, length us, event | category | flops | bytes accessed | tf_op | source)
XLA Modules:
  0.0 249.6 jit_solution(1443142181651891734)
XLA Ops:
  0.6 0.0 copy-start
  0.6 0.6 copy-done
  1.3 0.0 copy-start.4
  1.3 0.9 copy-done.4
  2.2 0.0 copy-start.5
  2.2 0.9 copy-done.5
  3.2 0.0 copy-start.6
  3.2 0.7 copy-done.6
  3.8 0.0 copy-start.3
  3.8 0.6 shard_map.85
  4.5 139.8 %all_to_all.10 = bf16[64,8,1024]{2,1,0:T(8,128)(2,1)S(1)} all-to-all(bf16[64,8,1024]{2,1,0:T(8,128)(2,1)S(1)} %bitcast.14), channel_id=1, replica_groups=mesh['dp'=16,'expert'=64] {'expert'}, dimensions={0} | all-to-all | bytes 2097152 | tf_op jit(solution)/shard_map/all_to_all | solution.py:146
  144.3 0.0 copy-done.3
  144.3 0.0 copy-start.2
  144.3 2.2 copy-done.2
  146.5 2.4 shard_map.86
  148.9 0.0 copy-start.7
  148.9 1.3 copy-done.7
  150.3 0.0 copy-start.9
  150.3 0.8 copy-done.9
  151.1 0.0 copy-start.11
  151.1 0.8 copy-done.11
  151.9 1.0 reshape.28
  152.8 5.5 %all-to-all-start.1 = ((bf16[64,4,1024]{2,1,0:T(4,128)(2,1)}), bf16[64,4,1024]{2,1,0:T(4,128)(2,1)}, u32[]{:S(2)}, u32[]{:S(2)}) async-start(bf16[64,4,1024]{2,1,0:T(4,128)(2,1)} %reshape.28), calls=%async_computation.1 | async-start | bytes 1048576 | tf_op jit(solution)/shard_map/all_to_all | solution.py:161
  158.4 0.1 pad_add_fusion.me_ref
  158.4 0.0 copy-start.8
  158.4 1.6 copy-done.8
  160.0 0.0 copy-start.10
  160.0 1.0 copy-done.10
  161.1 0.0 copy-start.12
  161.1 1.0 copy-done.12
  162.1 3.5 %shard_map.87 = (bf16[4,64,1536]{2,1,0:T(8,128)(2,1)S(1)}, bf16[4,64,1536]{2,1,0:T(8,128)(2,1)S(1)}, bf16[4,64,1536]{2,1,0:T(8,128)(2,1)S(1)}, bf16[4,64,1536]{2...) custom-call(s32[2]{0:T(128)S(1)} %pad_add_fusion.me_ref, ...), custom_call_target="tpu_custom_call" | custom-call | flops 2147483648 | bytes 16777216 | tf_op jit(solution)/shard_map/pallas_call | solution.py:167
  165.7 2.4 collective-permute-start
  168.1 4.3 %collective-permute-start.1 = (bf16[4,64,1536]{2,1,0:T(8,128)(2,1)S(1)}, bf16[4,64,1536]{2,1,0:T(8,128)(2,1)S(1)}, u32[]{:S(2)}, u32[]{:S(2)}) collective-permute-start(bf16[4,64,1536]{2,1,0:T(8,128)(2,1)S(1)} %get-tuple-element.37), channel_id=1, source_target_pairs={{0,128},{64,192},{128,0},{192,64},{256,384},{320,448},{384,256},{4... | collective-permute-start | bytes 2359304 | tf_op jit(solution)/shard_map/ppermute | solution.py:177
  172.4 1.9 collective-permute-start.2
  174.3 3.5 %collective-permute-start.3 = (bf16[4,64,1536]{2,1,0:T(8,128)(2,1)S(1)}, bf16[4,64,1536]{2,1,0:T(8,128)(2,1)S(1)}, u32[]{:S(2)}, u32[]{:S(2)}) collective-permute-start(bf16[4,64,1536]{2,1,0:T(8,128)(2,1)S(1)} %get-tuple-element.40), channel_id=1, source_target_pairs={{0,256},{64,320},{128,384},{192,448},{256,512},{320,576},{384,640}... | collective-permute-start | bytes 2359304 | tf_op jit(solution)/shard_map/ppermute | solution.py:180
  177.8 4.8 %collective-permute-start.4 = (bf16[4,64,1536]{2,1,0:T(8,128)(2,1)S(1)}, bf16[4,64,1536]{2,1,0:T(8,128)(2,1)S(1)}, u32[]{:S(2)}, u32[]{:S(2)}) collective-permute-start(bf16[4,64,1536]{2,1,0:T(8,128)(2,1)S(1)} %get-tuple-element.41), channel_id=1, source_target_pairs={{0,512},{64,576},{128,640},{192,704},{256,768},{320,832},{384,896}... | collective-permute-start | bytes 2359304 | tf_op jit(solution)/shard_map/ppermute | solution.py:180
  182.6 5.4 %collective-permute-done.refs_1_ = bf16[4,64,1536]{2,1,0:T(8,128)(2,1)S(1)} collective-permute-done((bf16[4,64,1536]{2,1,0:T(8,128)(2,1)S(1)}, bf16[4,64,1536]{2,1,0:T(8,128)(2,1)S(1)}, u32[]{:S(2)}, u32[]{:S(2)}) %collective-permute-start) | collective-permute-done | bytes 786464 | tf_op jit(solution)/shard_map/ppermute | solution.py:177
  188.0 4.9 %collective-permute-start.5 = (bf16[4,64,1536]{2,1,0:T(8,128)(2,1)S(1)}, bf16[4,64,1536]{2,1,0:T(8,128)(2,1)S(1)}, u32[]{:S(2)}, u32[]{:S(2)}) collective-permute-start(bf16[4,64,1536]{2,1,0:T(8,128)(2,1)S(1)} %get-tuple-element.42), channel_id=1, source_target_pairs={{0,768},{64,832},{128,896},{192,960},{256,0},{320,64},{384,128},{4... | collective-permute-start | bytes 2359304 | tf_op jit(solution)/shard_map/ppermute | solution.py:180
  192.9 0.0 collective-permute-done.1.refs_2_
  192.9 14.4 %collective-permute-done.2.refs_3_ = bf16[4,64,1536]{2,1,0:T(8,128)(2,1)S(1)} collective-permute-done((bf16[4,64,1536]{2,1,0:T(8,128)(2,1)S(1)}, bf16[4,64,1536]{2,1,0:T(8,128)(2,1)S(1)}, u32[]{:S(2)}, u32[]{:S(2)}) %collective-permute-start.2) | collective-permute-done | bytes 786464 | tf_op jit(solution)/shard_map/ppermute | solution.py:177
  207.3 0.0 collective-permute-done.3.refs_5_
  207.3 6.9 %collective-permute-done.4.refs_6_ = bf16[4,64,1536]{2,1,0:T(8,128)(2,1)S(1)} collective-permute-done((bf16[4,64,1536]{2,1,0:T(8,128)(2,1)S(1)}, bf16[4,64,1536]{2,1,0:T(8,128)(2,1)S(1)}, u32[]{:S(2)}, u32[]{:S(2)}) %collective-permute-start.4) | collective-permute-done | bytes 786464 | tf_op jit(solution)/shard_map/ppermute | solution.py:180
  214.2 1.4 collective-permute-done.5.refs_7_
  215.6 1.3 shard_map.88
  216.9 0.0 copy-start.1
  216.9 4.4 %collective-permute-start.6 = (bf16[64,1536]{1,0:T(8,128)(2,1)S(1)}, bf16[64,1536]{1,0:T(8,128)(2,1)S(1)}, u32[]{:S(2)}, u32[]{:S(2)}) collective-permute-start(bf16[64,1536]{1,0:T(8,128)(2,1)S(1)} %get-tuple-element.44), channel_id=1, source_target_pairs={{0,256},{64,320},{128,384},{192,448},{256,512},{320,576},{384,640}... | collective-permute-start | bytes 589832 | tf_op jit(solution)/shard_map/ppermute | solution.py:180
  221.3 3.5 %collective-permute-start.7 = (bf16[64,1536]{1,0:T(8,128)(2,1)S(1)}, bf16[64,1536]{1,0:T(8,128)(2,1)S(1)}, u32[]{:S(2)}, u32[]{:S(2)}) collective-permute-start(bf16[64,1536]{1,0:T(8,128)(2,1)S(1)} %get-tuple-element.45), channel_id=1, source_target_pairs={{0,512},{64,576},{128,640},{192,704},{256,768},{320,832},{384,896}... | collective-permute-start | bytes 589832 | tf_op jit(solution)/shard_map/ppermute | solution.py:180
  224.9 3.6 %collective-permute-start.8 = (bf16[64,1536]{1,0:T(8,128)(2,1)S(1)}, bf16[64,1536]{1,0:T(8,128)(2,1)S(1)}, u32[]{:S(2)}, u32[]{:S(2)}) collective-permute-start(bf16[64,1536]{1,0:T(8,128)(2,1)S(1)} %get-tuple-element.46), channel_id=1, source_target_pairs={{0,768},{64,832},{128,896},{192,960},{256,0},{320,64},{384,128},{4... | collective-permute-start | bytes 589832 | tf_op jit(solution)/shard_map/ppermute | solution.py:180
  228.4 4.9 %collective-permute-start.9 = (bf16[64,1536]{1,0:T(8,128)(2,1)S(1)}, bf16[64,1536]{1,0:T(8,128)(2,1)S(1)}, u32[]{:S(2)}, u32[]{:S(2)}) collective-permute-start(bf16[64,1536]{1,0:T(8,128)(2,1)S(1)} %get-tuple-element.48), channel_id=1, source_target_pairs={{0,64},{64,128},{128,192},{192,0},{256,320},{320,384},{384,448},{4... | collective-permute-start | bytes 589832 | tf_op jit(solution)/shard_map/ppermute | solution.py:177
  233.3 2.0 collective-permute-start.10
  235.3 0.0 collective-permute-done.6.refs_1_
  235.3 3.3 %collective-permute-start.11 = (bf16[64,1536]{1,0:T(8,128)(2,1)S(1)}, bf16[64,1536]{1,0:T(8,128)(2,1)S(1)}, u32[]{:S(2)}, u32[]{:S(2)}) collective-permute-start(bf16[64,1536]{1,0:T(8,128)(2,1)S(1)} %get-tuple-element.50), channel_id=1, source_target_pairs={{0,192},{64,0},{128,64},{192,128},{256,448},{320,256},{384,320},{4... | collective-permute-start | bytes 589832 | tf_op jit(solution)/shard_map/ppermute | solution.py:177
  238.6 0.0 collective-permute-done.7.refs_2_
  238.6 0.0 collective-permute-done.8.refs_3_
  238.6 2.2 collective-permute-done.9.refs_5_
  240.8 3.5 %collective-permute-done.10.refs_6_ = bf16[64,1536]{1,0:T(8,128)(2,1)S(1)} collective-permute-done((bf16[64,1536]{1,0:T(8,128)(2,1)S(1)}, bf16[64,1536]{1,0:T(8,128)(2,1)S(1)}, u32[]{:S(2)}, u32[]{:S(2)}) %collective-permute-start.10) | collective-permute-done | bytes 196640 | tf_op jit(solution)/shard_map/ppermute | solution.py:177
  244.3 2.1 collective-permute-done.11.refs_7_
  246.4 1.0 shard_map.89
  247.4 0.0 all-to-all-done.1
  247.4 1.2 reshape.29
  248.6 0.0 copy-done.1
  248.6 1.0 fusion
Async XLA Ops:
  0.6 0.7 copy-start
  1.3 0.9 copy-start.4
  2.2 0.9 copy-start.5
  3.2 0.7 copy-start.6
  3.8 140.5 %copy-start.3 = (bf16[1,1024,1024]{2,1,0:T(8,128)(2,1)S(1)}, bf16[1,1024,1024]{2,1,0:T(8,128)(2,1)}, u32[]{:S(2)}) copy-start(bf16[1,1024,1024]{2,1,0:T(8,128)(2,1)} %param.11) | copy-start | bytes 6291460
  144.3 2.2 copy-start.2
  148.9 1.3 copy-start.7
  150.3 0.8 copy-start.9
  151.1 0.8 copy-start.11
  152.8 94.6 %all-to-all-start.1 = ((bf16[64,4,1024]{2,1,0:T(4,128)(2,1)}), bf16[64,4,1024]{2,1,0:T(4,128)(2,1)}, u32[]{:S(2)}, u32[]{:S(2)}) async-start(bf16[64,4,1024]{2,1,0:T(4,128)(2,1)} %reshape.28), calls=%async_computation.1 | async-start | bytes 1048576 | tf_op jit(solution)/shard_map/all_to_all | solution.py:161
  158.4 1.6 copy-start.8
  160.0 1.0 copy-start.10
  161.1 1.0 copy-start.12
  165.7 22.3 %collective-permute-start = (bf16[4,64,1536]{2,1,0:T(8,128)(2,1)S(1)}, bf16[4,64,1536]{2,1,0:T(8,128)(2,1)S(1)}, u32[]{:S(2)}, u32[]{:S(2)}) collective-permute-start(bf16[4,64,1536]{2,1,0:T(8,128)(2,1)S(1)} %get-tuple-element.36), channel_id=1, source_target_pairs={{0,64},{64,128},{128,192},{192,0},{256,320},{320,384},{384,448},{4... | collective-permute-start | bytes 2359304 | tf_op jit(solution)/shard_map/ppermute | solution.py:177
  168.1 24.9 %collective-permute-start.1 = (bf16[4,64,1536]{2,1,0:T(8,128)(2,1)S(1)}, bf16[4,64,1536]{2,1,0:T(8,128)(2,1)S(1)}, u32[]{:S(2)}, u32[]{:S(2)}) collective-permute-start(bf16[4,64,1536]{2,1,0:T(8,128)(2,1)S(1)} %get-tuple-element.37), channel_id=1, source_target_pairs={{0,128},{64,192},{128,0},{192,64},{256,384},{320,448},{384,256},{4... | collective-permute-start | bytes 2359304 | tf_op jit(solution)/shard_map/ppermute | solution.py:177
  172.4 34.9 %collective-permute-start.2 = (bf16[4,64,1536]{2,1,0:T(8,128)(2,1)S(1)}, bf16[4,64,1536]{2,1,0:T(8,128)(2,1)S(1)}, u32[]{:S(2)}, u32[]{:S(2)}) collective-permute-start(bf16[4,64,1536]{2,1,0:T(8,128)(2,1)S(1)} %get-tuple-element.38), channel_id=1, source_target_pairs={{0,192},{64,0},{128,64},{192,128},{256,448},{320,256},{384,320},{4... | collective-permute-start | bytes 2359304 | tf_op jit(solution)/shard_map/ppermute | solution.py:177
  174.3 33.0 %collective-permute-start.3 = (bf16[4,64,1536]{2,1,0:T(8,128)(2,1)S(1)}, bf16[4,64,1536]{2,1,0:T(8,128)(2,1)S(1)}, u32[]{:S(2)}, u32[]{:S(2)}) collective-permute-start(bf16[4,64,1536]{2,1,0:T(8,128)(2,1)S(1)} %get-tuple-element.40), channel_id=1, source_target_pairs={{0,256},{64,320},{128,384},{192,448},{256,512},{320,576},{384,640}... | collective-permute-start | bytes 2359304 | tf_op jit(solution)/shard_map/ppermute | solution.py:180
  177.8 36.4 %collective-permute-start.4 = (bf16[4,64,1536]{2,1,0:T(8,128)(2,1)S(1)}, bf16[4,64,1536]{2,1,0:T(8,128)(2,1)S(1)}, u32[]{:S(2)}, u32[]{:S(2)}) collective-permute-start(bf16[4,64,1536]{2,1,0:T(8,128)(2,1)S(1)} %get-tuple-element.41), channel_id=1, source_target_pairs={{0,512},{64,576},{128,640},{192,704},{256,768},{320,832},{384,896}... | collective-permute-start | bytes 2359304 | tf_op jit(solution)/shard_map/ppermute | solution.py:180
  188.0 27.6 %collective-permute-start.5 = (bf16[4,64,1536]{2,1,0:T(8,128)(2,1)S(1)}, bf16[4,64,1536]{2,1,0:T(8,128)(2,1)S(1)}, u32[]{:S(2)}, u32[]{:S(2)}) collective-permute-start(bf16[4,64,1536]{2,1,0:T(8,128)(2,1)S(1)} %get-tuple-element.42), channel_id=1, source_target_pairs={{0,768},{64,832},{128,896},{192,960},{256,0},{320,64},{384,128},{4... | collective-permute-start | bytes 2359304 | tf_op jit(solution)/shard_map/ppermute | solution.py:180
  216.9 31.7 %copy-start.1 = (f32[128,1]{0,1:T(1,128)S(1)}, f32[128,1]{0,1:T(1,128)}, u32[]{:S(2)}) copy-start(f32[128,1]{0,1:T(1,128)} %param.9) | copy-start | bytes 1540
  216.9 18.3 %collective-permute-start.6 = (bf16[64,1536]{1,0:T(8,128)(2,1)S(1)}, bf16[64,1536]{1,0:T(8,128)(2,1)S(1)}, u32[]{:S(2)}, u32[]{:S(2)}) collective-permute-start(bf16[64,1536]{1,0:T(8,128)(2,1)S(1)} %get-tuple-element.44), channel_id=1, source_target_pairs={{0,256},{64,320},{128,384},{192,448},{256,512},{320,576},{384,640}... | collective-permute-start | bytes 589832 | tf_op jit(solution)/shard_map/ppermute | solution.py:180
  221.3 17.3 %collective-permute-start.7 = (bf16[64,1536]{1,0:T(8,128)(2,1)S(1)}, bf16[64,1536]{1,0:T(8,128)(2,1)S(1)}, u32[]{:S(2)}, u32[]{:S(2)}) collective-permute-start(bf16[64,1536]{1,0:T(8,128)(2,1)S(1)} %get-tuple-element.45), channel_id=1, source_target_pairs={{0,512},{64,576},{128,640},{192,704},{256,768},{320,832},{384,896}... | collective-permute-start | bytes 589832 | tf_op jit(solution)/shard_map/ppermute | solution.py:180
  224.9 13.8 %collective-permute-start.8 = (bf16[64,1536]{1,0:T(8,128)(2,1)S(1)}, bf16[64,1536]{1,0:T(8,128)(2,1)S(1)}, u32[]{:S(2)}, u32[]{:S(2)}) collective-permute-start(bf16[64,1536]{1,0:T(8,128)(2,1)S(1)} %get-tuple-element.46), channel_id=1, source_target_pairs={{0,768},{64,832},{128,896},{192,960},{256,0},{320,64},{384,128},{4... | collective-permute-start | bytes 589832 | tf_op jit(solution)/shard_map/ppermute | solution.py:180
  228.4 12.3 %collective-permute-start.9 = (bf16[64,1536]{1,0:T(8,128)(2,1)S(1)}, bf16[64,1536]{1,0:T(8,128)(2,1)S(1)}, u32[]{:S(2)}, u32[]{:S(2)}) collective-permute-start(bf16[64,1536]{1,0:T(8,128)(2,1)S(1)} %get-tuple-element.48), channel_id=1, source_target_pairs={{0,64},{64,128},{128,192},{192,0},{256,320},{320,384},{384,448},{4... | collective-permute-start | bytes 589832 | tf_op jit(solution)/shard_map/ppermute | solution.py:177
  233.3 11.0 %collective-permute-start.10 = (bf16[64,1536]{1,0:T(8,128)(2,1)S(1)}, bf16[64,1536]{1,0:T(8,128)(2,1)S(1)}, u32[]{:S(2)}, u32[]{:S(2)}) collective-permute-start(bf16[64,1536]{1,0:T(8,128)(2,1)S(1)} %get-tuple-element.49), channel_id=1, source_target_pairs={{0,128},{64,192},{128,0},{192,64},{256,384},{320,448},{384,256},{4... | collective-permute-start | bytes 589832 | tf_op jit(solution)/shard_map/ppermute | solution.py:177
  235.3 11.1 %collective-permute-start.11 = (bf16[64,1536]{1,0:T(8,128)(2,1)S(1)}, bf16[64,1536]{1,0:T(8,128)(2,1)S(1)}, u32[]{:S(2)}, u32[]{:S(2)}) collective-permute-start(bf16[64,1536]{1,0:T(8,128)(2,1)S(1)} %get-tuple-element.50), channel_id=1, source_target_pairs={{0,192},{64,0},{128,64},{192,128},{256,448},{320,256},{384,320},{4... | collective-permute-start | bytes 589832 | tf_op jit(solution)/shard_map/ppermute | solution.py:177

commit v2 on v1

v2 whole, which is shorter than its diff:
```python
import functools
import jax
import jax.numpy as jnp
from jax import lax
from jax.experimental import pallas as pl
from jax.experimental.pallas import tpu as pltpu
from jax.sharding import PartitionSpec as P

BF = jnp.bfloat16
F32 = jnp.float32
MIB = 1 << 20
RING = 4


def call(body, outs, flops, moved, n_in, vmem=12, scratch=(), hbm=0, out_hbm=False):
    vm = pl.BlockSpec(memory_space=pltpu.VMEM)
    far = pl.BlockSpec(memory_space=pltpu.HBM)
    return pl.pallas_call(
        body,
        out_shape=[jax.ShapeDtypeStruct(s, t) for s, t in outs],
        in_specs=[far] * hbm + [vm] * (n_in - hbm),
        out_specs=[far if out_hbm else vm] * len(outs),
        scratch_shapes=list(scratch),
        compiler_params=pltpu.CompilerParams(vmem_limit_bytes=vmem * MIB),
        cost_estimate=pl.CostEstimate(flops=flops, bytes_accessed=moved, transcendentals=0),
    )


def dot(a, b, dims):
    return lax.dot_general(a, b, (dims, ((), ())), preferred_element_type=F32)


def place_kernel(cap, x_hbm, c_hbm, r_hbm, g_hbm, send_ref, pos_ref, x_ref, c_ref, r_ref, g_ref, sems):
    pairs = ((r_hbm, r_ref), (g_hbm, g_ref), (x_hbm, x_ref), (c_hbm, c_ref))
    copies = [pltpu.make_async_copy(a, b, sems.at[i]) for i, (a, b) in enumerate(pairs)]
    for copy in copies:
        copy.start()
    for copy in copies:
        copy.wait()
    tok = x_ref.shape[0]
    r = jnp.broadcast_to(r_ref[...], (tok, tok))
    g = jnp.transpose(jnp.broadcast_to(g_ref[...], (tok, tok)))[:, :1]
    row = lax.broadcasted_iota(jnp.int32, (tok, tok), 0)
    col = lax.broadcasted_iota(jnp.int32, (tok, tok), 1)
    same = jnp.where((jnp.transpose(r) == r) & (row < col), 1, 0)
    slot = jnp.sum(same, axis=0, keepdims=True)
    route = r_ref[...]
    pos_ref[...] = route * cap + slot
    at = route * (2 * cap) + slot
    at = jnp.concatenate([at, at + cap], axis=1)
    rows = lax.broadcasted_iota(jnp.int32, (send_ref.shape[0], 2 * tok), 0)
    placing = jnp.where(rows == at, 1.0, 0.0).astype(BF)
    dy = (g * c_ref[...].astype(F32)).astype(BF)
    both = jnp.concatenate([x_ref[...], dy], axis=0)
    send_ref[...] = dot(placing, both, ((1,), (0,))).astype(BF)


STEP = 512


def weight_copies(wi_hbm, wo_hbm, wi_ref, wo_ref, sems):
    hidden = wo_hbm.shape[1]
    pieces = [pl.ds(at, STEP) for h in range(0, hidden, STEP) for at in (h, hidden + h)]
    copies = [
        pltpu.make_async_copy(wi_hbm.at[:, cols], wi_ref.at[:, cols], sems.at[i])
        for i, cols in enumerate(pieces)
    ]
    last = pltpu.make_async_copy(wo_hbm, wo_ref, sems.at[len(copies)])
    for copy in copies:
        copy.start()
    last.start()
    return copies, last


def expert_kernel(cap, wi_hbm, wo_hbm, got_hbm, y_hbm, *refs):
    a, b = refs[:RING], refs[RING : 2 * RING]
    wi_ref, wo_ref, got_ref, y_ref, hid_ref, da_ref, acc_ref, w_sems, sems, out_sems = refs[2 * RING :]
    arrival = pltpu.make_async_copy(got_hbm, got_ref, sems.at[0])
    arrival.start()
    copies, last = weight_copies(wi_hbm, wo_hbm, wi_ref, wo_ref, w_sems)
    n, hidden = hid_ref.shape
    r = lax.broadcasted_iota(jnp.int32, (n, 2 * n), 0)
    c = lax.broadcasted_iota(jnp.int32, (n, 2 * n), 1)
    at = (r // cap) * (2 * cap) + r % cap
    arrival.wait()
    got = got_ref[...]
    x = dot(jnp.where(c == at, 1.0, 0.0).astype(BF), got, ((1,), (0,))).astype(BF)
    dy = dot(jnp.where(c == at + cap, 1.0, 0.0).astype(BF), got, ((1,), (0,))).astype(BF)
    for h in range(0, hidden, STEP):
        copies[2 * h // STEP].wait()
        g = dot(x, wi_ref[:, h : h + STEP], ((1,), (0,)))
        copies[2 * h // STEP + 1].wait()
        u = dot(x, wi_ref[:, hidden + h : hidden + h + STEP], ((1,), (0,)))
        sig = jax.nn.sigmoid(g)
        swish = g * sig
        hid_ref[:, h : h + STEP] = (swish * u).astype(BF)
        if h == 0:
            last.wait()
        dh = dot(dy, wo_ref[:, h : h + STEP], ((1,), (0,)))
        da_ref[:, h : h + STEP] = (dh * u * sig * (1.0 + g * (1.0 - sig))).astype(BF)
        da_ref[:, hidden + h : hidden + h + STEP] = (dh * swish).astype(BF)
    y = dot(hid_ref[...], wo_ref[...], ((1,), (1,)))
    y_ref[...] = y.reshape(y_ref.shape).astype(BF)
    outs = [pltpu.make_async_copy(y_ref, y_hbm, sems.at[1])]
    outs[0].start()
    x_t, dy_t = jnp.transpose(x), jnp.transpose(dy)
    me = lax.axis_index("dp")
    me_y, me_x = me // RING, me % RING
    block = x.shape[1] // RING
    share = block // RING
    cols = hidden + hidden // 2
    for y_at in range(RING):
        rows = slice(y_at * block, (y_at + 1) * block)
        for k in range(2):
            acc_ref[y_at, :, k * cols : k * cols + hidden] = dot(
                x_t[rows], da_ref[:, k * hidden : (k + 1) * hidden], ((1,), (0,))
            ).astype(BF)
            acc_ref[y_at, :, k * cols + hidden : (k + 1) * cols] = dot(
                dy_t[rows], hid_ref[:, k * hidden // 2 : (k + 1) * hidden // 2], ((1,), (0,))
            ).astype(BF)
        for k in range(RING):
            at = pl.multiple_of(((me_x + k) % RING) * share, share)
            outs.append(
                pltpu.make_async_copy(
                    acc_ref.at[y_at, pl.ds(at, share), pl.ds(0, cols)],
                    a[k].at[y_at],
                    out_sems.at[0, y_at, k],
                )
            )
            outs[-1].start()
    for k in range(RING):
        at = (me_y + k) % RING
        for x_at in range(RING):
            outs.append(
                pltpu.make_async_copy(
                    acc_ref.at[at, pl.ds(x_at * share, share), pl.ds(cols, cols)],
                    b[k].at[x_at],
                    out_sems.at[1, k, x_at],
                )
            )
            outs[-1].start()
    for copy in outs:
        copy.wait()


def middle_kernel(axis, *refs):
    parts, outs = refs[:RING], refs[RING:]
    me = lax.axis_index("dp")
    me = me // RING if axis == 0 else me % RING
    for t in range(RING):
        at = (me + t) % RING
        total = parts[0][at].astype(F32)
        for part in parts[1:]:
            total = total + part[at].astype(F32)
        outs[t][...] = total.astype(outs[t].dtype)


def last_kernel(*refs):
    a, b = refs[:RING], refs[RING : 2 * RING]
    in_ref, out_ref = refs[2 * RING :]
    half_in, half_out = in_ref.shape[1] // 2, out_ref.shape[1] // 2
    for k, parts in enumerate((a, b)):
        total = parts[0][...]
        for part in parts[1:]:
            total = total + part[...].astype(F32)
        in_ref[:, k * half_in : (k + 1) * half_in] = total[:, :half_in]
        out_ref[:, k * half_out : (k + 1) * half_out] = total[:, half_in:]


def output_kernel(back_ref, pos_ref, g_ref, out_ref):
    tok = out_ref.shape[0]
    experts, cap, width = back_ref.shape
    g = jnp.transpose(jnp.broadcast_to(g_ref[...], (tok, tok)))[:, :1]
    rows = lax.broadcasted_iota(jnp.int32, (experts * cap, tok), 0)
    placing = jnp.where(rows == pos_ref[...], 1.0, 0.0).astype(BF)
    back = back_ref[...].astype(F32).reshape(experts * cap, width).astype(BF)
    out_ref[...] = (g * dot(placing, back, ((0,), (0,)))).astype(BF)


def on_device(latent, cotangent, routes, gates, w_in, w_out):
    n_experts = lax.axis_size("expert")
    tok, width = latent.shape
    hidden = w_out.shape[2]
    cap = max(2, 2 * tok // n_experts)
    rows = n_experts * cap
    gate_row = gates.reshape(1, tok)

    send, pos = call(
        functools.partial(place_kernel, cap),
        [((2 * rows, width), BF), ((1, tok), jnp.int32)],
        4 * rows * tok * width * 2, 4 * MIB, 4, hbm=4, vmem=62,
        scratch=[
            pltpu.VMEM((tok, width), BF),
            pltpu.VMEM((tok, width), BF),
            pltpu.VMEM((1, tok), jnp.int32),
            pltpu.VMEM((1, tok), F32),
            pltpu.SemaphoreType.DMA((4,)),
        ],
    )(latent, cotangent, routes.reshape(1, tok), gate_row)
    got = lax.all_to_all(
        send.reshape(n_experts, 2 * cap, width), "expert", split_axis=0, concat_axis=0, tiled=True
    ).reshape(2 * rows, width)

    share = width // (RING * RING)
    cols = hidden + hidden // 2
    y_buf, *parts = call(
        functools.partial(expert_kernel, cap),
        [((n_experts, cap, width), BF)] + [((RING, share, cols), BF)] * (2 * RING),
        2 * rows * width * hidden * 8, 16 * MIB, 3, hbm=3, vmem=58, out_hbm=True,
        scratch=[
            pltpu.VMEM((width, 2 * hidden), BF),
            pltpu.VMEM((width, hidden), BF),
            pltpu.VMEM((2 * rows, width), BF),
            pltpu.VMEM((n_experts, cap, width), BF),
            pltpu.VMEM((rows, hidden), BF),
            pltpu.VMEM((rows, 2 * hidden), BF),
            pltpu.VMEM((RING, width // RING, 2 * cols), BF),
            pltpu.SemaphoreType.DMA((2 * hidden // STEP + 1,)),
            pltpu.SemaphoreType.DMA((2,)),
            pltpu.SemaphoreType.DMA((2, RING, RING)),
        ],
    )(w_in[0], w_out[0], got)
    back = lax.all_to_all(y_buf, "expert", split_axis=0, concat_axis=0, tiled=True)

    def shift(v, dy, dx):
        ring = range(RING)
        pairs = [
            (RING * y + x, RING * ((y + dy) % RING) + (x + dx) % RING) for y in ring for x in ring
        ]
        return lax.ppermute(v, "dp", pairs)

    a, b = parts[:RING], parts[RING:]
    for k in range(1, RING):
        a[k] = shift(a[k], 0, k)
        b[k] = shift(b[k], k, 0)
    sums = [((share, cols), F32)] + [((share, cols), BF)] * (RING - 1)
    ends = []
    for axis, half in enumerate((a, b)):
        mids = call(
            functools.partial(middle_kernel, axis), sums, 8 * MIB, 5 * MIB, RING
        )(half[0], half[2], half[1], half[3])
        far = [shift(mids[t], t, 0) if axis == 0 else shift(mids[t], 0, t) for t in (1, 2, 3)]
        ends += [mids[0]] + far
    grad_in, grad_out = call(
        last_kernel,
        [((share, 2 * hidden), F32), ((share, hidden), F32)],
        4 * MIB, 4 * MIB, 2 * RING,
    )(*ends)

    (output,) = call(
        output_kernel, [((tok, width), BF)], 2 * rows * tok * width, MIB, 3
    )(back, pos, gate_row)
    return output, grad_in[None], grad_out[None]


def solution(mesh):
    tokens = P(("dp", "expert"), None)
    return jax.shard_map(
        on_device,
        mesh=mesh,
        in_specs=(tokens,) * 4 + (P("expert", None, None),) * 2,
        out_specs=(tokens, P("expert", "dp", None), P("expert", "dp", None)),
        check_vma=False,
    )
```

time: 250 us -> 232 us (0.928)
  local copies, waits for them, and re-layouts: 14.2 us -> 1.15 us
  waiting for transfers between devices: 35.8 us -> 25.1 us
  Pallas kernels: 8.85 us -> 16 us
    unnamed x26 -> x8, local copies, waits for them, and re-layouts: 12 us -> 1.15 us
    ppermute x12, waiting for transfers between devices: 35.8 us -> 25.1 us  [shift(): return lax.ppermute(v, 'dp', pairs)]
    pallas_call x3 -> x4, Pallas kernels: 7.22 us -> 12.3 us  [the longest x1 10.5 us: on_device(): call(functools.partial(expert_kernel, cap), [((n_experts, cap, width), BF...]
  transfers between devices with their start and end apart: 13 -> 13, of which waited for: 7 -> 6; matrix products, arithmetic and copies ran while one was open for 0% -> 0% of each run, Pallas kernels for 2% -> 1%
where the time goes in v2:
time: 232 us; the launch traced here: 230 us
  blocking collectives  140 us (60%)
  starting transfers between devices  46.8 us (20%)
  waiting for transfers between devices  25.1 us (11%)
  Pallas kernels  16 us (7%)
    all_to_all x1, blocking collectives, on_device(): lax.all_to_all(send.reshape(n_experts, 2 * cap, width), 'expert', split_a...  140 us
    ppermute x12, starting transfers between devices, shift(): return lax.ppermute(v, 'dp', pairs)  42 us
    ppermute x12, waiting for transfers between devices, shift(): return lax.ppermute(v, 'dp', pairs)  25.1 us
    pallas_call x1, Pallas kernels, on_device(): call(functools.partial(expert_kernel, cap), [((n_experts, cap, width), BF...  10.5 us
    all_to_all x1, starting transfers between devices, on_device(): lax.all_to_all(y_buf, 'expert', split_axis=0, concat_axis=0, tiled=True)  4.78 us
  transfers between devices with their start and end apart: 13, of which 6 were waited for; matrix products, arithmetic and copies ran while one was open for 0% of the time, Pallas kernels for 1%

profile of v2, /device:TPU:6, one launch (start us, length us, event | category | flops | bytes accessed | tf_op | source)
XLA Modules:
  0.0 230.0 jit_solution(2667204951072167574)
XLA Ops:
  0.6 2.7 %shard_map.85 = (bf16[512,1024]{1,0:T(8,128)(2,1)}, s32[1,128]{1,0:T(1,128)}) custom-call(bf16[128,1024]{1,0:T(8,128)(2,1)} %x_hbm.1, bf16[128,1024]{1,0:T(8,128)(2,1)} %c_hbm.1, s32[1,128]{1,0:T(1,128)} %bitcast.16, f32[1,128]{1,0:T(1,128)} %bitcast.8), custom_call_target="tpu_custom_call" | custom-call | flops 268435456 | bytes 4194304 | tf_op jit(solution)/shard_map/pallas_call | solution.py:188
  3.3 140.2 %all_to_all.10 = bf16[64,8,1024]{2,1,0:T(8,128)(2,1)} all-to-all(bf16[64,8,1024]{2,1,0:T(8,128)(2,1)} %bitcast.11), channel_id=1, replica_groups=mesh['dp'=16,'expert'=64] {'expert'}, dimensions={0} | all-to-all | bytes 2097152 | tf_op jit(solution)/shard_map/all_to_all | solution.py:200
  143.5 10.5 %shard_map.86 = (bf16[64,4,1024]{2,1,0:T(4,128)(2,1)}, bf16[4,64,1536]{2,1,0:T(8,128)(2,1)}, bf16[4,64,1536]{2,1,0:T(8,128)(2,1)}, bf16[4,64,1536]{2,1,0:T(8,128...) custom-call(bf16[1024,2048]{1,0:T(8,128)(2,1)} %bitcast.12, ...), custom_call_target="tpu_custom_call" | custom-call | flops 4294967296 | bytes 16777216 | tf_op jit(solution)/shard_map/pallas_call | solution.py:206
  154.0 0.0 copy-start
  154.0 4.8 %all-to-all-start.1 = ((bf16[64,4,1024]{2,1,0:T(4,128)(2,1)}), bf16[64,4,1024]{2,1,0:T(4,128)(2,1)S(1)}, u32[]{:S(2)}, u32[]{:S(2)}) async-start(bf16[64,4,1024]{2,1,0:T(4,128)(2,1)} %get-tuple-element.25), calls=%async_computation.1 | async-start | bytes 1048576 | tf_op jit(solution)/shard_map/all_to_all | solution.py:223
  158.8 0.0 copy-start.2
  158.8 0.0 copy-start.3
  158.8 3.3 %collective-permute-start = (bf16[4,64,1536]{2,1,0:T(8,128)(2,1)}, bf16[4,64,1536]{2,1,0:T(8,128)(2,1)S(1)}, u32[]{:S(2)}, u32[]{:S(2)}) collective-permute-start(bf16[4,64,1536]{2,1,0:T(8,128)(2,1)} %get-tuple-element.28), channel_id=1, source_target_pairs={{0,128},{64,192},{128,0},{192,64},{256,384},{320,448},{384,256},{4... | collective-permute-start | bytes 2359304 | tf_op jit(solution)/shard_map/ppermute | solution.py:230
  162.1 4.0 %collective-permute-start.1 = (bf16[4,64,1536]{2,1,0:T(8,128)(2,1)}, bf16[4,64,1536]{2,1,0:T(8,128)(2,1)S(1)}, u32[]{:S(2)}, u32[]{:S(2)}) collective-permute-start(bf16[4,64,1536]{2,1,0:T(8,128)(2,1)} %get-tuple-element.29), channel_id=1, source_target_pairs={{0,64},{64,128},{128,192},{192,0},{256,320},{320,384},{384,448},{4... | collective-permute-start | bytes 2359304 | tf_op jit(solution)/shard_map/ppermute | solution.py:230
  166.2 1.9 collective-permute-start.2
  168.1 5.1 %collective-permute-start.6 = (bf16[4,64,1536]{2,1,0:T(8,128)(2,1)}, bf16[4,64,1536]{2,1,0:T(8,128)(2,1)S(1)}, u32[]{:S(2)}, u32[]{:S(2)}) collective-permute-start(bf16[4,64,1536]{2,1,0:T(8,128)(2,1)} %get-tuple-element.36), channel_id=1, source_target_pairs={{0,512},{64,576},{128,640},{192,704},{256,768},{320,832},{384,896}... | collective-permute-start | bytes 2359304 | tf_op jit(solution)/shard_map/ppermute | solution.py:230
  173.2 2.6 %collective-permute-start.7 = (bf16[4,64,1536]{2,1,0:T(8,128)(2,1)}, bf16[4,64,1536]{2,1,0:T(8,128)(2,1)S(1)}, u32[]{:S(2)}, u32[]{:S(2)}) collective-permute-start(bf16[4,64,1536]{2,1,0:T(8,128)(2,1)} %get-tuple-element.37), channel_id=1, source_target_pairs={{0,256},{64,320},{128,384},{192,448},{256,512},{320,576},{384,640}... | collective-permute-start | bytes 2359304 | tf_op jit(solution)/shard_map/ppermute | solution.py:230
  175.8 7.1 %collective-permute-done.refs_1_ = bf16[4,64,1536]{2,1,0:T(8,128)(2,1)S(1)} collective-permute-done((bf16[4,64,1536]{2,1,0:T(8,128)(2,1)}, bf16[4,64,1536]{2,1,0:T(8,128)(2,1)S(1)}, u32[]{:S(2)}, u32[]{:S(2)}) %collective-permute-start) | collective-permute-done | bytes 786464 | tf_op jit(solution)/shard_map/ppermute | solution.py:230
  182.9 4.9 %collective-permute-start.8 = (bf16[4,64,1536]{2,1,0:T(8,128)(2,1)}, bf16[4,64,1536]{2,1,0:T(8,128)(2,1)S(1)}, u32[]{:S(2)}, u32[]{:S(2)}) collective-permute-start(bf16[4,64,1536]{2,1,0:T(8,128)(2,1)} %get-tuple-element.38), channel_id=1, source_target_pairs={{0,768},{64,832},{128,896},{192,960},{256,0},{320,64},{384,128},{4... | collective-permute-start | bytes 2359304 | tf_op jit(solution)/shard_map/ppermute | solution.py:230
  187.8 8.7 %collective-permute-done.1.refs_2_ = bf16[4,64,1536]{2,1,0:T(8,128)(2,1)S(1)} collective-permute-done((bf16[4,64,1536]{2,1,0:T(8,128)(2,1)}, bf16[4,64,1536]{2,1,0:T(8,128)(2,1)S(1)}, u32[]{:S(2)}, u32[]{:S(2)}) %collective-permute-start.1) | collective-permute-done | bytes 786464 | tf_op jit(solution)/shard_map/ppermute | solution.py:230
  196.5 2.2 collective-permute-done.2.refs_3_
  198.7 0.0 copy-start.1
  198.7 1.1 copy-done.1
  199.8 0.4 shard_map.88
  200.2 3.5 %collective-permute-start.3 = (bf16[64,1536]{1,0:T(8,128)(2,1)S(1)}, bf16[64,1536]{1,0:T(8,128)(2,1)S(1)}, u32[]{:S(2)}, u32[]{:S(2)}) collective-permute-start(bf16[64,1536]{1,0:T(8,128)(2,1)S(1)} %get-tuple-element.32), channel_id=1, source_target_pairs={{0,256},{64,320},{128,384},{192,448},{256,512},{320,576},{384,640}... | collective-permute-start | bytes 589832 | tf_op jit(solution)/shard_map/ppermute | solution.py:230
  203.7 4.8 %collective-permute-start.4 = (bf16[64,1536]{1,0:T(8,128)(2,1)S(1)}, bf16[64,1536]{1,0:T(8,128)(2,1)S(1)}, u32[]{:S(2)}, u32[]{:S(2)}) collective-permute-start(bf16[64,1536]{1,0:T(8,128)(2,1)S(1)} %get-tuple-element.33), channel_id=1, source_target_pairs={{0,512},{64,576},{128,640},{192,704},{256,768},{320,832},{384,896}... | collective-permute-start | bytes 589832 | tf_op jit(solution)/shard_map/ppermute | solution.py:230
  208.5 0.0 collective-permute-done.6.refs_1_
  208.5 3.3 %collective-permute-start.5 = (bf16[64,1536]{1,0:T(8,128)(2,1)S(1)}, bf16[64,1536]{1,0:T(8,128)(2,1)S(1)}, u32[]{:S(2)}, u32[]{:S(2)}) collective-permute-start(bf16[64,1536]{1,0:T(8,128)(2,1)S(1)} %get-tuple-element.34), channel_id=1, source_target_pairs={{0,768},{64,832},{128,896},{192,960},{256,0},{320,64},{384,128},{4... | collective-permute-start | bytes 589832 | tf_op jit(solution)/shard_map/ppermute | solution.py:230
  211.8 0.0 collective-permute-done.7.refs_2_
  211.8 0.0 collective-permute-done.8.refs_3_
  211.8 0.0 copy-done
  211.8 0.4 shard_map.89
  212.2 2.5 %collective-permute-start.9 = (bf16[64,1536]{1,0:T(8,128)(2,1)S(1)}, bf16[64,1536]{1,0:T(8,128)(2,1)S(1)}, u32[]{:S(2)}, u32[]{:S(2)}) collective-permute-start(bf16[64,1536]{1,0:T(8,128)(2,1)S(1)} %get-tuple-element.40), channel_id=1, source_target_pairs={{0,64},{64,128},{128,192},{192,0},{256,320},{320,384},{384,448},{4... | collective-permute-start | bytes 589832 | tf_op jit(solution)/shard_map/ppermute | solution.py:230
  214.8 4.2 %collective-permute-start.10 = (bf16[64,1536]{1,0:T(8,128)(2,1)S(1)}, bf16[64,1536]{1,0:T(8,128)(2,1)S(1)}, u32[]{:S(2)}, u32[]{:S(2)}) collective-permute-start(bf16[64,1536]{1,0:T(8,128)(2,1)S(1)} %get-tuple-element.41), channel_id=1, source_target_pairs={{0,128},{64,192},{128,0},{192,64},{256,384},{320,448},{384,256},{4... | collective-permute-start | bytes 589832 | tf_op jit(solution)/shard_map/ppermute | solution.py:230
  218.9 0.0 collective-permute-done.3.refs_1_
  219.0 1.9 collective-permute-start.11
  220.9 0.0 collective-permute-done.4.refs_2_
  220.9 0.0 collective-permute-done.5.refs_3_
  220.9 1.0 collective-permute-done.9.refs_5_
  221.9 2.4 %collective-permute-done.10.refs_6_ = bf16[64,1536]{1,0:T(8,128)(2,1)S(1)} collective-permute-done((bf16[64,1536]{1,0:T(8,128)(2,1)S(1)}, bf16[64,1536]{1,0:T(8,128)(2,1)S(1)}, u32[]{:S(2)}, u32[]{:S(2)}) %collective-permute-start.10) | collective-permute-done | bytes 196640 | tf_op jit(solution)/shard_map/ppermute | solution.py:230
  224.3 3.8 %collective-permute-done.11.refs_7_ = bf16[64,1536]{1,0:T(8,128)(2,1)S(1)} collective-permute-done((bf16[64,1536]{1,0:T(8,128)(2,1)S(1)}, bf16[64,1536]{1,0:T(8,128)(2,1)S(1)}, u32[]{:S(2)}, u32[]{:S(2)}) %collective-permute-start.11) | collective-permute-done | bytes 196640 | tf_op jit(solution)/shard_map/ppermute | solution.py:230
  228.0 1.0 shard_map.90
  229.0 0.0 all-to-all-done.1.back_ref
  229.0 0.0 copy-done.2
  229.0 0.0 copy-done.3
  229.0 1.0 shard_map.87
Async XLA Ops:
  154.0 57.8 %copy-start = (bf16[4,64,1536]{2,1,0:T(8,128)(2,1)S(1)}, bf16[4,64,1536]{2,1,0:T(8,128)(2,1)}, u32[]{:S(2)}) copy-start(bf16[4,64,1536]{2,1,0:T(8,128)(2,1)} %get-tuple-element.35.refs_0_) | copy-start | bytes 2359300
  154.0 75.0 %all-to-all-start.1 = ((bf16[64,4,1024]{2,1,0:T(4,128)(2,1)}), bf16[64,4,1024]{2,1,0:T(4,128)(2,1)S(1)}, u32[]{:S(2)}, u32[]{:S(2)}) async-start(bf16[64,4,1024]{2,1,0:T(4,128)(2,1)} %get-tuple-element.25), calls=%async_computation.1 | async-start | bytes 1048576 | tf_op jit(solution)/shard_map/all_to_all | solution.py:223
  158.8 70.2 %copy-start.2 = (f32[128,1]{0,1:T(1,128)S(1)}, f32[128,1]{0,1:T(1,128)}, u32[]{:S(2)}) copy-start(f32[128,1]{0,1:T(1,128)} %param.9) | copy-start | bytes 1540
  158.8 70.2 %copy-start.3 = (s32[1,128]{1,0:T(1,128)S(1)}, s32[1,128]{1,0:T(1,128)}, u32[]{:S(2)}) copy-start(s32[1,128]{1,0:T(1,128)} %get-tuple-element.26.pos_ref) | copy-start | bytes 1540
  158.8 24.1 %collective-permute-start = (bf16[4,64,1536]{2,1,0:T(8,128)(2,1)}, bf16[4,64,1536]{2,1,0:T(8,128)(2,1)S(1)}, u32[]{:S(2)}, u32[]{:S(2)}) collective-permute-start(bf16[4,64,1536]{2,1,0:T(8,128)(2,1)} %get-tuple-element.28), channel_id=1, source_target_pairs={{0,128},{64,192},{128,0},{192,64},{256,384},{320,448},{384,256},{4... | collective-permute-start | bytes 2359304 | tf_op jit(solution)/shard_map/ppermute | solution.py:230
  162.1 34.4 %collective-permute-start.1 = (bf16[4,64,1536]{2,1,0:T(8,128)(2,1)}, bf16[4,64,1536]{2,1,0:T(8,128)(2,1)S(1)}, u32[]{:S(2)}, u32[]{:S(2)}) collective-permute-start(bf16[4,64,1536]{2,1,0:T(8,128)(2,1)} %get-tuple-element.29), channel_id=1, source_target_pairs={{0,64},{64,128},{128,192},{192,0},{256,320},{320,384},{384,448},{4... | collective-permute-start | bytes 2359304 | tf_op jit(solution)/shard_map/ppermute | solution.py:230
  166.2 32.5 %collective-permute-start.2 = (bf16[4,64,1536]{2,1,0:T(8,128)(2,1)}, bf16[4,64,1536]{2,1,0:T(8,128)(2,1)S(1)}, u32[]{:S(2)}, u32[]{:S(2)}) collective-permute-start(bf16[4,64,1536]{2,1,0:T(8,128)(2,1)} %get-tuple-element.30), channel_id=1, source_target_pairs={{0,192},{64,0},{128,64},{192,128},{256,448},{320,256},{384,320},{4... | collective-permute-start | bytes 2359304 | tf_op jit(solution)/shard_map/ppermute | solution.py:230
  168.1 40.4 %collective-permute-start.6 = (bf16[4,64,1536]{2,1,0:T(8,128)(2,1)}, bf16[4,64,1536]{2,1,0:T(8,128)(2,1)S(1)}, u32[]{:S(2)}, u32[]{:S(2)}) collective-permute-start(bf16[4,64,1536]{2,1,0:T(8,128)(2,1)} %get-tuple-element.36), channel_id=1, source_target_pairs={{0,512},{64,576},{128,640},{192,704},{256,768},{320,832},{384,896}... | collective-permute-start | bytes 2359304 | tf_op jit(solution)/shard_map/ppermute | solution.py:230
  173.2 38.6 %collective-permute-start.7 = (bf16[4,64,1536]{2,1,0:T(8,128)(2,1)}, bf16[4,64,1536]{2,1,0:T(8,128)(2,1)S(1)}, u32[]{:S(2)}, u32[]{:S(2)}) collective-permute-start(bf16[4,64,1536]{2,1,0:T(8,128)(2,1)} %get-tuple-element.37), channel_id=1, source_target_pairs={{0,256},{64,320},{128,384},{192,448},{256,512},{320,576},{384,640}... | collective-permute-start | bytes 2359304 | tf_op jit(solution)/shard_map/ppermute | solution.py:230
  182.9 28.9 %collective-permute-start.8 = (bf16[4,64,1536]{2,1,0:T(8,128)(2,1)}, bf16[4,64,1536]{2,1,0:T(8,128)(2,1)S(1)}, u32[]{:S(2)}, u32[]{:S(2)}) collective-permute-start(bf16[4,64,1536]{2,1,0:T(8,128)(2,1)} %get-tuple-element.38), channel_id=1, source_target_pairs={{0,768},{64,832},{128,896},{192,960},{256,0},{320,64},{384,128},{4... | collective-permute-start | bytes 2359304 | tf_op jit(solution)/shard_map/ppermute | solution.py:230
  198.7 1.1 copy-start.1
  200.2 18.7 %collective-permute-start.3 = (bf16[64,1536]{1,0:T(8,128)(2,1)S(1)}, bf16[64,1536]{1,0:T(8,128)(2,1)S(1)}, u32[]{:S(2)}, u32[]{:S(2)}) collective-permute-start(bf16[64,1536]{1,0:T(8,128)(2,1)S(1)} %get-tuple-element.32), channel_id=1, source_target_pairs={{0,256},{64,320},{128,384},{192,448},{256,512},{320,576},{384,640}... | collective-permute-start | bytes 589832 | tf_op jit(solution)/shard_map/ppermute | solution.py:230
  203.7 17.2 %collective-permute-start.4 = (bf16[64,1536]{1,0:T(8,128)(2,1)S(1)}, bf16[64,1536]{1,0:T(8,128)(2,1)S(1)}, u32[]{:S(2)}, u32[]{:S(2)}) collective-permute-start(bf16[64,1536]{1,0:T(8,128)(2,1)S(1)} %get-tuple-element.33), channel_id=1, source_target_pairs={{0,512},{64,576},{128,640},{192,704},{256,768},{320,832},{384,896}... | collective-permute-start | bytes 589832 | tf_op jit(solution)/shard_map/ppermute | solution.py:230
  208.5 12.4 %collective-permute-start.5 = (bf16[64,1536]{1,0:T(8,128)(2,1)S(1)}, bf16[64,1536]{1,0:T(8,128)(2,1)S(1)}, u32[]{:S(2)}, u32[]{:S(2)}) collective-permute-start(bf16[64,1536]{1,0:T(8,128)(2,1)S(1)} %get-tuple-element.34), channel_id=1, source_target_pairs={{0,768},{64,832},{128,896},{192,960},{256,0},{320,64},{384,128},{4... | collective-permute-start | bytes 589832 | tf_op jit(solution)/shard_map/ppermute | solution.py:230
  212.2 9.7 %collective-permute-start.9 = (bf16[64,1536]{1,0:T(8,128)(2,1)S(1)}, bf16[64,1536]{1,0:T(8,128)(2,1)S(1)}, u32[]{:S(2)}, u32[]{:S(2)}) collective-permute-start(bf16[64,1536]{1,0:T(8,128)(2,1)S(1)} %get-tuple-element.40), channel_id=1, source_target_pairs={{0,64},{64,128},{128,192},{192,0},{256,320},{320,384},{384,448},{4... | collective-permute-start | bytes 589832 | tf_op jit(solution)/shard_map/ppermute | solution.py:230
  214.8 9.5 %collective-permute-start.10 = (bf16[64,1536]{1,0:T(8,128)(2,1)S(1)}, bf16[64,1536]{1,0:T(8,128)(2,1)S(1)}, u32[]{:S(2)}, u32[]{:S(2)}) collective-permute-start(bf16[64,1536]{1,0:T(8,128)(2,1)S(1)} %get-tuple-element.41), channel_id=1, source_target_pairs={{0,128},{64,192},{128,0},{192,64},{256,384},{320,448},{384,256},{4... | collective-permute-start | bytes 589832 | tf_op jit(solution)/shard_map/ppermute | solution.py:230
  219.0 9.1 %collective-permute-start.11 = (bf16[64,1536]{1,0:T(8,128)(2,1)S(1)}, bf16[64,1536]{1,0:T(8,128)(2,1)S(1)}, u32[]{:S(2)}, u32[]{:S(2)}) collective-permute-start(bf16[64,1536]{1,0:T(8,128)(2,1)S(1)} %get-tuple-element.42), channel_id=1, source_target_pairs={{0,192},{64,0},{128,64},{192,128},{256,448},{320,256},{384,320},{4... | collective-permute-start | bytes 589832 | tf_op jit(solution)/shard_map/ppermute | solution.py:230

commit v3 on v2

--- a/solution.py
+++ b/solution.py
@@ -66,23 +66,25 @@
         for i, cols in enumerate(pieces)
     ]
     last = pltpu.make_async_copy(wo_hbm, wo_ref, sems.at[len(copies)])
-    for copy in copies:
-        copy.start()
-    last.start()
     return copies, last
 
 
 def expert_kernel(cap, wi_hbm, wo_hbm, got_hbm, y_hbm, *refs):
     a, b = refs[:RING], refs[RING : 2 * RING]
-    wi_ref, wo_ref, got_ref, y_ref, hid_ref, da_ref, acc_ref, w_sems, sems, out_sems = refs[2 * RING :]
+    wi_ref, wo_ref, got_ref, y_ref, hid_ref, da_ref, xt_ref, dyt_ref, acc_ref, w_sems, sems, out_sems = refs[2 * RING :]
     arrival = pltpu.make_async_copy(got_hbm, got_ref, sems.at[0])
     arrival.start()
     copies, last = weight_copies(wi_hbm, wo_hbm, wi_ref, wo_ref, w_sems)
+    copies[0].start()
+    copies[1].start()
     n, hidden = hid_ref.shape
-    r = lax.broadcasted_iota(jnp.int32, (n, 2 * n), 0)
+    r = lax.broadcasted_iota(jnp.int32, (n, 1), 0)
     c = lax.broadcasted_iota(jnp.int32, (n, 2 * n), 1)
     at = (r // cap) * (2 * cap) + r % cap
     arrival.wait()
+    last.start()
+    for copy in copies[2:]:
+        copy.start()
     got = got_ref[...]
     x = dot(jnp.where(c == at, 1.0, 0.0).astype(BF), got, ((1,), (0,))).astype(BF)
     dy = dot(jnp.where(c == at + cap, 1.0, 0.0).astype(BF), got, ((1,), (0,))).astype(BF)
@@ -103,42 +105,33 @@
     y_ref[...] = y.reshape(y_ref.shape).astype(BF)
     outs = [pltpu.make_async_copy(y_ref, y_hbm, sems.at[1])]
     outs[0].start()
-    x_t, dy_t = jnp.transpose(x), jnp.transpose(dy)
+    xt_ref[...] = jnp.transpose(x)
+    dyt_ref[...] = jnp.transpose(dy)
     me = lax.axis_index("dp")
     me_y, me_x = me // RING, me % RING
     block = x.shape[1] // RING
     share = block // RING
     cols = hidden + hidden // 2
-    for y_at in range(RING):
-        rows = slice(y_at * block, (y_at + 1) * block)
-        for k in range(2):
-            acc_ref[y_at, :, k * cols : k * cols + hidden] = dot(
-                x_t[rows], da_ref[:, k * hidden : (k + 1) * hidden], ((1,), (0,))
+    for j in range(RING):
+        y_at = (me_y + j) % RING
+        rows = pl.ds(pl.multiple_of(y_at * block, block), block)
+        for half, pieces in enumerate((a, b)):
+            acc_ref[j, :, half * cols : half * cols + hidden] = dot(
+                xt_ref[rows, :], da_ref[:, half * hidden : (half + 1) * hidden], ((1,), (0,))
             ).astype(BF)
-            acc_ref[y_at, :, k * cols + hidden : (k + 1) * cols] = dot(
-                dy_t[rows], hid_ref[:, k * hidden // 2 : (k + 1) * hidden // 2], ((1,), (0,))
+            acc_ref[j, :, half * cols + hidden : (half + 1) * cols] = dot(
+                dyt_ref[rows, :], hid_ref[:, half * hidden // 2 : (half + 1) * hidden // 2], ((1,), (0,))
             ).astype(BF)
-        for k in range(RING):
-            at = pl.multiple_of(((me_x + k) % RING) * share, share)
-            outs.append(
-                pltpu.make_async_copy(
-                    acc_ref.at[y_at, pl.ds(at, share), pl.ds(0, cols)],
-                    a[k].at[y_at],
-                    out_sems.at[0, y_at, k],
-                )
-            )
-            outs[-1].start()
-    for k in range(RING):
-        at = (me_y + k) % RING
-        for x_at in range(RING):
-            outs.append(
-                pltpu.make_async_copy(
-                    acc_ref.at[at, pl.ds(x_at * share, share), pl.ds(cols, cols)],
-                    b[k].at[x_at],
-                    out_sems.at[1, k, x_at],
-                )
-            )
-            outs[-1].start()
+            for k in range(RING):
+                if half == 0:
+                    at = pl.multiple_of(((me_x + k) % RING) * share, share)
+                    target = a[k].at[y_at]
+                else:
+                    at = k * share
+                    target = b[j].at[k]
+                source = acc_ref.at[j, pl.ds(at, share), pl.ds(half * cols, cols)]
+                outs.append(pltpu.make_async_copy(source, target, out_sems.at[half, j, k]))
+                outs[-1].start()
     for copy in outs:
         copy.wait()
 
@@ -214,6 +207,8 @@
             pltpu.VMEM((n_experts, cap, width), BF),
             pltpu.VMEM((rows, hidden), BF),
             pltpu.VMEM((rows, 2 * hidden), BF),
+            pltpu.VMEM((width, rows), BF),
+            pltpu.VMEM((width, rows), BF),
             pltpu.VMEM((RING, width // RING, 2 * cols), BF),
             pltpu.SemaphoreType.DMA((2 * hidden // STEP + 1,)),
             pltpu.SemaphoreType.DMA((2,)),
@@ -239,7 +234,7 @@
         mids = call(
             functools.partial(middle_kernel, axis), sums, 8 * MIB, 5 * MIB, RING
         )(half[0], half[2], half[1], half[3])
-        far = [shift(mids[t], t, 0) if axis == 0 else shift(mids[t], 0, t) for t in (1, 2, 3)]
+        far = [shift(mids[t], t, 0) if axis == 0 else shift(mids[t], 0, t) for t in (2, 1, 3)]
         ends += [mids[0]] + far
     grad_in, grad_out = call(
         last_kernel,

time: 232 us -> 230 us (level)
  no operation moved by 1% of the time
where the time goes in v3:
time: 230 us; the launch traced here: 229 us
  blocking collectives  140 us (61%)
  starting transfers between devices  48 us (21%)
  waiting for transfers between devices  24.8 us (11%)
  Pallas kernels  14.4 us (6%)
    all_to_all x1, blocking collectives, on_device(): lax.all_to_all(send.reshape(n_experts, 2 * cap, width), 'expert', split_a...  140 us
    ppermute x12, starting transfers between devices, shift(): return lax.ppermute(v, 'dp', pairs)  43.2 us
    ppermute x12, waiting for transfers between devices, shift(): return lax.ppermute(v, 'dp', pairs)  24.8 us
    pallas_call x1, Pallas kernels, on_device(): call(functools.partial(expert_kernel, cap), [((n_experts, cap, width), BF...  8.94 us
    all_to_all x1, starting transfers between devices, on_device(): lax.all_to_all(y_buf, 'expert', split_axis=0, concat_axis=0, tiled=True)  4.78 us
  transfers between devices with their start and end apart: 13, of which 6 were waited for; matrix products, arithmetic and copies ran while one was open for 0% of the time, Pallas kernels for 1%

profile of v3, /device:TPU:6, one launch (start us, length us, event | category | flops | bytes accessed | tf_op | source)
XLA Modules:
  0.0 229.4 jit_solution(17549657750920397999)
XLA Ops:
  0.6 2.7 %shard_map.85 = (bf16[512,1024]{1,0:T(8,128)(2,1)}, s32[1,128]{1,0:T(1,128)}) custom-call(bf16[128,1024]{1,0:T(8,128)(2,1)} %x_hbm.1, bf16[128,1024]{1,0:T(8,128)(2,1)} %c_hbm.1, s32[1,128]{1,0:T(1,128)} %bitcast.16, f32[1,128]{1,0:T(1,128)} %bitcast.8), custom_call_target="tpu_custom_call" | custom-call | flops 268435456 | bytes 4194304 | tf_op jit(solution)/shard_map/pallas_call | solution.py:181
  3.3 140.2 %all_to_all.10 = bf16[64,8,1024]{2,1,0:T(8,128)(2,1)} all-to-all(bf16[64,8,1024]{2,1,0:T(8,128)(2,1)} %bitcast.11), channel_id=1, replica_groups=mesh['dp'=16,'expert'=64] {'expert'}, dimensions={0} | all-to-all | bytes 2097152 | tf_op jit(solution)/shard_map/all_to_all | solution.py:193
  143.5 8.9 %shard_map.86 = (bf16[64,4,1024]{2,1,0:T(4,128)(2,1)}, bf16[4,64,1536]{2,1,0:T(8,128)(2,1)}, bf16[4,64,1536]{2,1,0:T(8,128)(2,1)}, bf16[4,64,1536]{2,1,0:T(8,128...) custom-call(bf16[1024,2048]{1,0:T(8,128)(2,1)} %bitcast.12, ...), custom_call_target="tpu_custom_call" | custom-call | flops 4294967296 | bytes 16777216 | tf_op jit(solution)/shard_map/pallas_call | solution.py:199
  152.4 0.0 copy-start
  152.4 4.8 %all-to-all-start.1 = ((bf16[64,4,1024]{2,1,0:T(4,128)(2,1)}), bf16[64,4,1024]{2,1,0:T(4,128)(2,1)S(1)}, u32[]{:S(2)}, u32[]{:S(2)}) async-start(bf16[64,4,1024]{2,1,0:T(4,128)(2,1)} %get-tuple-element.25), calls=%async_computation.1 | async-start | bytes 1048576 | tf_op jit(solution)/shard_map/all_to_all | solution.py:218
  157.2 0.0 copy-start.2
  157.2 0.0 copy-start.3
  157.3 3.3 %collective-permute-start = (bf16[4,64,1536]{2,1,0:T(8,128)(2,1)}, bf16[4,64,1536]{2,1,0:T(8,128)(2,1)S(1)}, u32[]{:S(2)}, u32[]{:S(2)}) collective-permute-start(bf16[4,64,1536]{2,1,0:T(8,128)(2,1)} %get-tuple-element.28), channel_id=1, source_target_pairs={{0,128},{64,192},{128,0},{192,64},{256,384},{320,448},{384,256},{4... | collective-permute-start | bytes 2359304 | tf_op jit(solution)/shard_map/ppermute | solution.py:225
  160.6 4.0 %collective-permute-start.1 = (bf16[4,64,1536]{2,1,0:T(8,128)(2,1)}, bf16[4,64,1536]{2,1,0:T(8,128)(2,1)S(1)}, u32[]{:S(2)}, u32[]{:S(2)}) collective-permute-start(bf16[4,64,1536]{2,1,0:T(8,128)(2,1)} %get-tuple-element.29), channel_id=1, source_target_pairs={{0,64},{64,128},{128,192},{192,0},{256,320},{320,384},{384,448},{4... | collective-permute-start | bytes 2359304 | tf_op jit(solution)/shard_map/ppermute | solution.py:225
  164.6 1.9 collective-permute-start.2
  166.5 5.1 %collective-permute-start.6 = (bf16[4,64,1536]{2,1,0:T(8,128)(2,1)}, bf16[4,64,1536]{2,1,0:T(8,128)(2,1)S(1)}, u32[]{:S(2)}, u32[]{:S(2)}) collective-permute-start(bf16[4,64,1536]{2,1,0:T(8,128)(2,1)} %get-tuple-element.36), channel_id=1, source_target_pairs={{0,512},{64,576},{128,640},{192,704},{256,768},{320,832},{384,896}... | collective-permute-start | bytes 2359304 | tf_op jit(solution)/shard_map/ppermute | solution.py:225
  171.7 2.5 %collective-permute-start.7 = (bf16[4,64,1536]{2,1,0:T(8,128)(2,1)}, bf16[4,64,1536]{2,1,0:T(8,128)(2,1)S(1)}, u32[]{:S(2)}, u32[]{:S(2)}) collective-permute-start(bf16[4,64,1536]{2,1,0:T(8,128)(2,1)} %get-tuple-element.37), channel_id=1, source_target_pairs={{0,256},{64,320},{128,384},{192,448},{256,512},{320,576},{384,640}... | collective-permute-start | bytes 2359304 | tf_op jit(solution)/shard_map/ppermute | solution.py:225
  174.2 7.1 %collective-permute-done.refs_1_ = bf16[4,64,1536]{2,1,0:T(8,128)(2,1)S(1)} collective-permute-done((bf16[4,64,1536]{2,1,0:T(8,128)(2,1)}, bf16[4,64,1536]{2,1,0:T(8,128)(2,1)S(1)}, u32[]{:S(2)}, u32[]{:S(2)}) %collective-permute-start) | collective-permute-done | bytes 786464 | tf_op jit(solution)/shard_map/ppermute | solution.py:225
  181.3 4.9 %collective-permute-start.8 = (bf16[4,64,1536]{2,1,0:T(8,128)(2,1)}, bf16[4,64,1536]{2,1,0:T(8,128)(2,1)S(1)}, u32[]{:S(2)}, u32[]{:S(2)}) collective-permute-start(bf16[4,64,1536]{2,1,0:T(8,128)(2,1)} %get-tuple-element.38), channel_id=1, source_target_pairs={{0,768},{64,832},{128,896},{192,960},{256,0},{320,64},{384,128},{4... | collective-permute-start | bytes 2359304 | tf_op jit(solution)/shard_map/ppermute | solution.py:225
  186.2 8.7 %collective-permute-done.1.refs_2_ = bf16[4,64,1536]{2,1,0:T(8,128)(2,1)S(1)} collective-permute-done((bf16[4,64,1536]{2,1,0:T(8,128)(2,1)}, bf16[4,64,1536]{2,1,0:T(8,128)(2,1)S(1)}, u32[]{:S(2)}, u32[]{:S(2)}) %collective-permute-start.1) | collective-permute-done | bytes 786464 | tf_op jit(solution)/shard_map/ppermute | solution.py:225
  194.9 2.2 collective-permute-done.2.refs_3_
  197.1 0.0 copy-start.1
  197.1 1.1 copy-done.1
  198.2 0.4 shard_map.88
  198.6 5.1 %collective-permute-start.3 = (bf16[64,1536]{1,0:T(8,128)(2,1)S(1)}, bf16[64,1536]{1,0:T(8,128)(2,1)S(1)}, u32[]{:S(2)}, u32[]{:S(2)}) collective-permute-start(bf16[64,1536]{1,0:T(8,128)(2,1)S(1)} %get-tuple-element.32), channel_id=1, source_target_pairs={{0,512},{64,576},{128,640},{192,704},{256,768},{320,832},{384,896}... | collective-permute-start | bytes 589832 | tf_op jit(solution)/shard_map/ppermute | solution.py:225
  203.8 2.5 %collective-permute-start.4 = (bf16[64,1536]{1,0:T(8,128)(2,1)S(1)}, bf16[64,1536]{1,0:T(8,128)(2,1)S(1)}, u32[]{:S(2)}, u32[]{:S(2)}) collective-permute-start(bf16[64,1536]{1,0:T(8,128)(2,1)S(1)} %get-tuple-element.33), channel_id=1, source_target_pairs={{0,256},{64,320},{128,384},{192,448},{256,512},{320,576},{384,640}... | collective-permute-start | bytes 589832 | tf_op jit(solution)/shard_map/ppermute | solution.py:225
  206.3 0.0 collective-permute-done.6.refs_1_
  206.3 4.5 %collective-permute-start.5 = (bf16[64,1536]{1,0:T(8,128)(2,1)S(1)}, bf16[64,1536]{1,0:T(8,128)(2,1)S(1)}, u32[]{:S(2)}, u32[]{:S(2)}) collective-permute-start(bf16[64,1536]{1,0:T(8,128)(2,1)S(1)} %get-tuple-element.34), channel_id=1, source_target_pairs={{0,768},{64,832},{128,896},{192,960},{256,0},{320,64},{384,128},{4... | collective-permute-start | bytes 589832 | tf_op jit(solution)/shard_map/ppermute | solution.py:225
  210.8 0.0 collective-permute-done.7.refs_2_
  210.9 0.0 collective-permute-done.8.refs_3_
  210.9 0.0 copy-done
  210.9 0.4 shard_map.89
  211.3 3.4 %collective-permute-start.9 = (bf16[64,1536]{1,0:T(8,128)(2,1)S(1)}, bf16[64,1536]{1,0:T(8,128)(2,1)S(1)}, u32[]{:S(2)}, u32[]{:S(2)}) collective-permute-start(bf16[64,1536]{1,0:T(8,128)(2,1)S(1)} %get-tuple-element.40), channel_id=1, source_target_pairs={{0,128},{64,192},{128,0},{192,64},{256,384},{320,448},{384,256},{4... | collective-permute-start | bytes 589832 | tf_op jit(solution)/shard_map/ppermute | solution.py:225
  214.7 3.9 %collective-permute-start.10 = (bf16[64,1536]{1,0:T(8,128)(2,1)S(1)}, bf16[64,1536]{1,0:T(8,128)(2,1)S(1)}, u32[]{:S(2)}, u32[]{:S(2)}) collective-permute-start(bf16[64,1536]{1,0:T(8,128)(2,1)S(1)} %get-tuple-element.41), channel_id=1, source_target_pairs={{0,64},{64,128},{128,192},{192,0},{256,320},{320,384},{384,448},{4... | collective-permute-start | bytes 589832 | tf_op jit(solution)/shard_map/ppermute | solution.py:225
  218.6 0.0 collective-permute-done.3.refs_1_
  218.6 1.9 collective-permute-start.11
  220.6 0.0 collective-permute-done.4.refs_2_
  220.6 0.0 collective-permute-done.5.refs_3_
  220.6 0.1 collective-permute-done.9.refs_5_
  220.7 2.0 collective-permute-done.10.refs_6_
  222.7 4.7 %collective-permute-done.11.refs_7_ = bf16[64,1536]{1,0:T(8,128)(2,1)S(1)} collective-permute-done((bf16[64,1536]{1,0:T(8,128)(2,1)S(1)}, bf16[64,1536]{1,0:T(8,128)(2,1)S(1)}, u32[]{:S(2)}, u32[]{:S(2)}) %collective-permute-start.11) | collective-permute-done | bytes 196640 | tf_op jit(solution)/shard_map/ppermute | solution.py:225
  227.4 1.0 shard_map.90
  228.4 0.0 all-to-all-done.1.back_ref
  228.4 0.0 copy-done.2
  228.4 0.0 copy-done.3
  228.4 1.0 shard_map.87
Async XLA Ops:
  152.4 58.4 %copy-start = (bf16[4,64,1536]{2,1,0:T(8,128)(2,1)S(1)}, bf16[4,64,1536]{2,1,0:T(8,128)(2,1)}, u32[]{:S(2)}) copy-start(bf16[4,64,1536]{2,1,0:T(8,128)(2,1)} %get-tuple-element.35.refs_0_) | copy-start | bytes 2359300
  152.4 76.0 %all-to-all-start.1 = ((bf16[64,4,1024]{2,1,0:T(4,128)(2,1)}), bf16[64,4,1024]{2,1,0:T(4,128)(2,1)S(1)}, u32[]{:S(2)}, u32[]{:S(2)}) async-start(bf16[64,4,1024]{2,1,0:T(4,128)(2,1)} %get-tuple-element.25), calls=%async_computation.1 | async-start | bytes 1048576 | tf_op jit(solution)/shard_map/all_to_all | solution.py:218
  157.2 71.2 %copy-start.2 = (f32[128,1]{0,1:T(1,128)S(1)}, f32[128,1]{0,1:T(1,128)}, u32[]{:S(2)}) copy-start(f32[128,1]{0,1:T(1,128)} %param.9) | copy-start | bytes 1540
  157.2 71.2 %copy-start.3 = (s32[1,128]{1,0:T(1,128)S(1)}, s32[1,128]{1,0:T(1,128)}, u32[]{:S(2)}) copy-start(s32[1,128]{1,0:T(1,128)} %get-tuple-element.26.pos_ref) | copy-start | bytes 1540
  157.3 24.1 %collective-permute-start = (bf16[4,64,1536]{2,1,0:T(8,128)(2,1)}, bf16[4,64,1536]{2,1,0:T(8,128)(2,1)S(1)}, u32[]{:S(2)}, u32[]{:S(2)}) collective-permute-start(bf16[4,64,1536]{2,1,0:T(8,128)(2,1)} %get-tuple-element.28), channel_id=1, source_target_pairs={{0,128},{64,192},{128,0},{192,64},{256,384},{320,448},{384,256},{4... | collective-permute-start | bytes 2359304 | tf_op jit(solution)/shard_map/ppermute | solution.py:225
  160.6 34.4 %collective-permute-start.1 = (bf16[4,64,1536]{2,1,0:T(8,128)(2,1)}, bf16[4,64,1536]{2,1,0:T(8,128)(2,1)S(1)}, u32[]{:S(2)}, u32[]{:S(2)}) collective-permute-start(bf16[4,64,1536]{2,1,0:T(8,128)(2,1)} %get-tuple-element.29), channel_id=1, source_target_pairs={{0,64},{64,128},{128,192},{192,0},{256,320},{320,384},{384,448},{4... | collective-permute-start | bytes 2359304 | tf_op jit(solution)/shard_map/ppermute | solution.py:225
  164.6 32.5 %collective-permute-start.2 = (bf16[4,64,1536]{2,1,0:T(8,128)(2,1)}, bf16[4,64,1536]{2,1,0:T(8,128)(2,1)S(1)}, u32[]{:S(2)}, u32[]{:S(2)}) collective-permute-start(bf16[4,64,1536]{2,1,0:T(8,128)(2,1)} %get-tuple-element.30), channel_id=1, source_target_pairs={{0,192},{64,0},{128,64},{192,128},{256,448},{320,256},{384,320},{4... | collective-permute-start | bytes 2359304 | tf_op jit(solution)/shard_map/ppermute | solution.py:225
  166.5 39.8 %collective-permute-start.6 = (bf16[4,64,1536]{2,1,0:T(8,128)(2,1)}, bf16[4,64,1536]{2,1,0:T(8,128)(2,1)S(1)}, u32[]{:S(2)}, u32[]{:S(2)}) collective-permute-start(bf16[4,64,1536]{2,1,0:T(8,128)(2,1)} %get-tuple-element.36), channel_id=1, source_target_pairs={{0,512},{64,576},{128,640},{192,704},{256,768},{320,832},{384,896}... | collective-permute-start | bytes 2359304 | tf_op jit(solution)/shard_map/ppermute | solution.py:225
  171.7 39.2 %collective-permute-start.7 = (bf16[4,64,1536]{2,1,0:T(8,128)(2,1)}, bf16[4,64,1536]{2,1,0:T(8,128)(2,1)S(1)}, u32[]{:S(2)}, u32[]{:S(2)}) collective-permute-start(bf16[4,64,1536]{2,1,0:T(8,128)(2,1)} %get-tuple-element.37), channel_id=1, source_target_pairs={{0,256},{64,320},{128,384},{192,448},{256,512},{320,576},{384,640}... | collective-permute-start | bytes 2359304 | tf_op jit(solution)/shard_map/ppermute | solution.py:225
  181.3 29.5 %collective-permute-start.8 = (bf16[4,64,1536]{2,1,0:T(8,128)(2,1)}, bf16[4,64,1536]{2,1,0:T(8,128)(2,1)S(1)}, u32[]{:S(2)}, u32[]{:S(2)}) collective-permute-start(bf16[4,64,1536]{2,1,0:T(8,128)(2,1)} %get-tuple-element.38), channel_id=1, source_target_pairs={{0,768},{64,832},{128,896},{192,960},{256,0},{320,64},{384,128},{4... | collective-permute-start | bytes 2359304 | tf_op jit(solution)/shard_map/ppermute | solution.py:225
  197.1 1.1 copy-start.1
  198.6 20.0 %collective-permute-start.3 = (bf16[64,1536]{1,0:T(8,128)(2,1)S(1)}, bf16[64,1536]{1,0:T(8,128)(2,1)S(1)}, u32[]{:S(2)}, u32[]{:S(2)}) collective-permute-start(bf16[64,1536]{1,0:T(8,128)(2,1)S(1)} %get-tuple-element.32), channel_id=1, source_target_pairs={{0,512},{64,576},{128,640},{192,704},{256,768},{320,832},{384,896}... | collective-permute-start | bytes 589832 | tf_op jit(solution)/shard_map/ppermute | solution.py:225
  203.8 16.8 %collective-permute-start.4 = (bf16[64,1536]{1,0:T(8,128)(2,1)S(1)}, bf16[64,1536]{1,0:T(8,128)(2,1)S(1)}, u32[]{:S(2)}, u32[]{:S(2)}) collective-permute-start(bf16[64,1536]{1,0:T(8,128)(2,1)S(1)} %get-tuple-element.33), channel_id=1, source_target_pairs={{0,256},{64,320},{128,384},{192,448},{256,512},{320,576},{384,640}... | collective-permute-start | bytes 589832 | tf_op jit(solution)/shard_map/ppermute | solution.py:225
  206.3 14.2 %collective-permute-start.5 = (bf16[64,1536]{1,0:T(8,128)(2,1)S(1)}, bf16[64,1536]{1,0:T(8,128)(2,1)S(1)}, u32[]{:S(2)}, u32[]{:S(2)}) collective-permute-start(bf16[64,1536]{1,0:T(8,128)(2,1)S(1)} %get-tuple-element.34), channel_id=1, source_target_pairs={{0,768},{64,832},{128,896},{192,960},{256,0},{320,64},{384,128},{4... | collective-permute-start | bytes 589832 | tf_op jit(solution)/shard_map/ppermute | solution.py:225
  211.3 9.4 %collective-permute-start.9 = (bf16[64,1536]{1,0:T(8,128)(2,1)S(1)}, bf16[64,1536]{1,0:T(8,128)(2,1)S(1)}, u32[]{:S(2)}, u32[]{:S(2)}) collective-permute-start(bf16[64,1536]{1,0:T(8,128)(2,1)S(1)} %get-tuple-element.40), channel_id=1, source_target_pairs={{0,128},{64,192},{128,0},{192,64},{256,384},{320,448},{384,256},{4... | collective-permute-start | bytes 589832 | tf_op jit(solution)/shard_map/ppermute | solution.py:225
  214.7 8.0 %collective-permute-start.10 = (bf16[64,1536]{1,0:T(8,128)(2,1)S(1)}, bf16[64,1536]{1,0:T(8,128)(2,1)S(1)}, u32[]{:S(2)}, u32[]{:S(2)}) collective-permute-start(bf16[64,1536]{1,0:T(8,128)(2,1)S(1)} %get-tuple-element.41), channel_id=1, source_target_pairs={{0,64},{64,128},{128,192},{192,0},{256,320},{320,384},{384,448},{4... | collective-permute-start | bytes 589832 | tf_op jit(solution)/shard_map/ppermute | solution.py:225
  218.6 8.8 %collective-permute-start.11 = (bf16[64,1536]{1,0:T(8,128)(2,1)S(1)}, bf16[64,1536]{1,0:T(8,128)(2,1)S(1)}, u32[]{:S(2)}, u32[]{:S(2)}) collective-permute-start(bf16[64,1536]{1,0:T(8,128)(2,1)S(1)} %get-tuple-element.42), channel_id=1, source_target_pairs={{0,192},{64,0},{128,64},{192,128},{256,448},{320,256},{384,320},{4... | collective-permute-start | bytes 589832 | tf_op jit(solution)/shard_map/ppermute | solution.py:225

commit v4 on v3

--- a/solution.py
+++ b/solution.py
@@ -67,6 +67,11 @@
     ]
     last = pltpu.make_async_copy(wo_hbm, wo_ref, sems.at[len(copies)])
     return copies, last
+
+
+def half_columns(hidden):
+    few = 3 * hidden // 8
+    return few, hidden - few
 
 
 def expert_kernel(cap, wi_hbm, wo_hbm, got_hbm, y_hbm, *refs):
@@ -111,25 +116,28 @@
     me_y, me_x = me // RING, me % RING
     block = x.shape[1] // RING
     share = block // RING
-    cols = hidden + hidden // 2
+    cuts = half_columns(hidden)
     for j in range(RING):
         y_at = (me_y + j) % RING
         rows = pl.ds(pl.multiple_of(y_at * block, block), block)
         for half, pieces in enumerate((a, b)):
-            acc_ref[j, :, half * cols : half * cols + hidden] = dot(
+            first = cuts[0] + hidden if half else 0
+            outs_at = slice(cuts[0], hidden) if half else slice(0, cuts[0])
+            cols = hidden + cuts[half]
+            acc_ref[j, :, first : first + hidden] = dot(
                 xt_ref[rows, :], da_ref[:, half * hidden : (half + 1) * hidden], ((1,), (0,))
             ).astype(BF)
-            acc_ref[j, :, half * cols + hidden : (half + 1) * cols] = dot(
-                dyt_ref[rows, :], hid_ref[:, half * hidden // 2 : (half + 1) * hidden // 2], ((1,), (0,))
+            acc_ref[j, :, first + hidden : first + cols] = dot(
+                dyt_ref[rows, :], hid_ref[:, outs_at], ((1,), (0,))
             ).astype(BF)
             for k in range(RING):
                 if half == 0:
                     at = pl.multiple_of(((me_x + k) % RING) * share, share)
-                    target = a[k].at[y_at]
+                    target = pieces[k].at[y_at]
                 else:
                     at = k * share
-                    target = b[j].at[k]
-                source = acc_ref.at[j, pl.ds(at, share), pl.ds(half * cols, cols)]
+                    target = pieces[j].at[k]
+                source = acc_ref.at[j, pl.ds(at, share), pl.ds(first, cols)]
                 outs.append(pltpu.make_async_copy(source, target, out_sems.at[half, j, k]))
                 outs[-1].start()
     for copy in outs:
@@ -145,29 +153,32 @@
         total = parts[0][at].astype(F32)
         for part in parts[1:]:
             total = total + part[at].astype(F32)
-        outs[t][...] = total.astype(outs[t].dtype)
+        cols = total.shape[1]
+        outs[t][:, :cols] = total.astype(outs[t].dtype)
+        if cols < outs[t].shape[1]:
+            outs[t][:, cols:] = jnp.zeros((total.shape[0], outs[t].shape[1] - cols), outs[t].dtype)
 
 
 def last_kernel(*refs):
     a, b = refs[:RING], refs[RING : 2 * RING]
-    in_ref, out_ref = refs[2 * RING :]
-    half_in, half_out = in_ref.shape[1] // 2, out_ref.shape[1] // 2
+    back_ref, pos_ref, g_ref, y_ref, in_ref, out_ref = refs[2 * RING :]
+    half_in, few = in_ref.shape[1] // 2, half_columns(out_ref.shape[1])[0]
     for k, parts in enumerate((a, b)):
         total = parts[0][...]
         for part in parts[1:]:
             total = total + part[...].astype(F32)
         in_ref[:, k * half_in : (k + 1) * half_in] = total[:, :half_in]
-        out_ref[:, k * half_out : (k + 1) * half_out] = total[:, half_in:]
-
-
-def output_kernel(back_ref, pos_ref, g_ref, out_ref):
-    tok = out_ref.shape[0]
+        if k == 0:
+            out_ref[:, :few] = total[:, half_in : half_in + few]
+        else:
+            out_ref[:, few:] = total[:, half_in:]
+    tok = y_ref.shape[0]
     experts, cap, width = back_ref.shape
     g = jnp.transpose(jnp.broadcast_to(g_ref[...], (tok, tok)))[:, :1]
     rows = lax.broadcasted_iota(jnp.int32, (experts * cap, tok), 0)
     placing = jnp.where(rows == pos_ref[...], 1.0, 0.0).astype(BF)
     back = back_ref[...].astype(F32).reshape(experts * cap, width).astype(BF)
-    out_ref[...] = (g * dot(placing, back, ((0,), (0,)))).astype(BF)
+    y_ref[...] = (g * dot(placing, back, ((0,), (0,)))).astype(BF)
 
 
 def on_device(latent, cotangent, routes, gates, w_in, w_out):
@@ -195,10 +206,10 @@
     ).reshape(2 * rows, width)
 
     share = width // (RING * RING)
-    cols = hidden + hidden // 2
+    cols = [hidden + few for few in half_columns(hidden)]
     y_buf, *parts = call(
         functools.partial(expert_kernel, cap),
-        [((n_experts, cap, width), BF)] + [((RING, share, cols), BF)] * (2 * RING),
+        [((n_experts, cap, width), BF)] + [((RING, share, c), BF) for c in cols for _ in range(RING)],
         2 * rows * width * hidden * 8, 16 * MIB, 3, hbm=3, vmem=58, out_hbm=True,
         scratch=[
             pltpu.VMEM((width, 2 * hidden), BF),
@@ -209,7 +220,7 @@
             pltpu.VMEM((rows, 2 * hidden), BF),
             pltpu.VMEM((width, rows), BF),
             pltpu.VMEM((width, rows), BF),
-            pltpu.VMEM((RING, width // RING, 2 * cols), BF),
+            pltpu.VMEM((RING, width // RING, sum(cols)), BF),
             pltpu.SemaphoreType.DMA((2 * hidden // STEP + 1,)),
             pltpu.SemaphoreType.DMA((2,)),
             pltpu.SemaphoreType.DMA((2, RING, RING)),
@@ -228,23 +239,21 @@
     for k in range(1, RING):
         a[k] = shift(a[k], 0, k)
         b[k] = shift(b[k], k, 0)
-    sums = [((share, cols), F32)] + [((share, cols), BF)] * (RING - 1)
     ends = []
     for axis, half in enumerate((a, b)):
+        c = max(cols)
         mids = call(
-            functools.partial(middle_kernel, axis), sums, 8 * MIB, 5 * MIB, RING
+            functools.partial(middle_kernel, axis),
+            [((share, c), F32)] + [((share, c), BF)] * (RING - 1),
+            8 * MIB, 5 * MIB, RING,
         )(half[0], half[2], half[1], half[3])
         far = [shift(mids[t], t, 0) if axis == 0 else shift(mids[t], 0, t) for t in (2, 1, 3)]
         ends += [mids[0]] + far
-    grad_in, grad_out = call(
+    output, grad_in, grad_out = call(
         last_kernel,
-        [((share, 2 * hidden), F32), ((share, hidden), F32)],
-        4 * MIB, 4 * MIB, 2 * RING,
-    )(*ends)
-
-    (output,) = call(
-        output_kernel, [((tok, width), BF)], 2 * rows * tok * width, MIB, 3
-    )(back, pos, gate_row)
+        [((tok, width), BF), ((share, 2 * hidden), F32), ((share, hidden), F32)],
+        2 * rows * tok * width, 5 * MIB, 2 * RING + 3,
+    )(*ends, back, pos, gate_row)
     return output, grad_in[None], grad_out[None]
 
 

time: 230 us -> 232 us (level); the launches traced: 229 us -> 229 us
  transfers between devices with their start and end apart: 13 -> 13, of which waited for: 6 -> 8; matrix products, arithmetic and copies ran while one was open for 0% -> 0% of each run, Pallas kernels for 1% -> 0%
where the time goes in v4:
time: 232 us; the launch traced here: 229 us
  blocking collectives  140 us (60%)
  starting transfers between devices  48.6 us (21%)
  waiting for transfers between devices  24.6 us (11%)
  Pallas kernels  13.8 us (6%)
    all_to_all x1, blocking collectives, on_device(): lax.all_to_all(send.reshape(n_experts, 2 * cap, width), 'expert', split_a...  140 us
    ppermute x12, starting transfers between devices, shift(): return lax.ppermute(v, 'dp', pairs)  43.8 us
    ppermute x12, waiting for transfers between devices, shift(): return lax.ppermute(v, 'dp', pairs)  24.6 us
    pallas_call x1, Pallas kernels, on_device(): call(functools.partial(expert_kernel, cap), [((n_experts, cap, width), BF...  9.06 us
    all_to_all x1, starting transfers between devices, on_device(): lax.all_to_all(y_buf, 'expert', split_axis=0, concat_axis=0, tiled=True)  4.78 us
  transfers between devices with their start and end apart: 13, of which 8 were waited for; matrix products, arithmetic and copies ran while one was open for 0% of the time, Pallas kernels for 0%

profile of v4, /device:TPU:6, one launch (start us, length us, event | category | flops | bytes accessed | tf_op | source)
XLA Modules:
  0.0 229.0 jit_solution(9964177139143140578)
XLA Ops:
  0.6 2.7 %shard_map.85 = (bf16[512,1024]{1,0:T(8,128)(2,1)}, s32[1,128]{1,0:T(1,128)}) custom-call(bf16[128,1024]{1,0:T(8,128)(2,1)} %x_hbm.1, bf16[128,1024]{1,0:T(8,128)(2,1)} %c_hbm.1, s32[1,128]{1,0:T(1,128)} %bitcast.16, f32[1,128]{1,0:T(1,128)} %bitcast.8), custom_call_target="tpu_custom_call" | custom-call | flops 268435456 | bytes 4194304 | tf_op jit(solution)/shard_map/pallas_call | solution.py:192
  3.3 140.2 %all_to_all.10 = bf16[64,8,1024]{2,1,0:T(8,128)(2,1)} all-to-all(bf16[64,8,1024]{2,1,0:T(8,128)(2,1)} %bitcast.11), channel_id=1, replica_groups=mesh['dp'=16,'expert'=64] {'expert'}, dimensions={0} | all-to-all | bytes 2097152 | tf_op jit(solution)/shard_map/all_to_all | solution.py:204
  143.5 9.1 %shard_map.86 = (bf16[64,4,1024]{2,1,0:T(4,128)(2,1)}, bf16[4,64,1408]{2,1,0:T(8,128)(2,1)}, bf16[4,64,1408]{2,1,0:T(8,128)(2,1)}, bf16[4,64,1408]{2,1,0:T(8,128...) custom-call(bf16[1024,2048]{1,0:T(8,128)(2,1)} %bitcast.12, ...), custom_call_target="tpu_custom_call" | custom-call | flops 4294967296 | bytes 16777216 | tf_op jit(solution)/shard_map/pallas_call | solution.py:210
  152.6 0.0 copy-start
  152.6 0.0 copy-start.2
  152.6 0.0 copy-start.3
  152.6 4.8 %all-to-all-start.1 = ((bf16[64,4,1024]{2,1,0:T(4,128)(2,1)}), bf16[64,4,1024]{2,1,0:T(4,128)(2,1)S(1)}, u32[]{:S(2)}, u32[]{:S(2)}) async-start(bf16[64,4,1024]{2,1,0:T(4,128)(2,1)} %get-tuple-element.42), calls=%async_computation.1 | async-start | bytes 1048576 | tf_op jit(solution)/shard_map/all_to_all | solution.py:229
  157.4 3.3 %collective-permute-start = (bf16[4,64,1408]{2,1,0:T(8,128)(2,1)}, bf16[4,64,1408]{2,1,0:T(8,128)(2,1)S(1)}, u32[]{:S(2)}, u32[]{:S(2)}) collective-permute-start(bf16[4,64,1408]{2,1,0:T(8,128)(2,1)} %get-tuple-element.27), channel_id=1, source_target_pairs={{0,128},{64,192},{128,0},{192,64},{256,384},{320,448},{384,256},{4... | collective-permute-start | bytes 2162696 | tf_op jit(solution)/shard_map/ppermute | solution.py:236
  160.7 4.0 %collective-permute-start.1 = (bf16[4,64,1408]{2,1,0:T(8,128)(2,1)}, bf16[4,64,1408]{2,1,0:T(8,128)(2,1)S(1)}, u32[]{:S(2)}, u32[]{:S(2)}) collective-permute-start(bf16[4,64,1408]{2,1,0:T(8,128)(2,1)} %get-tuple-element.28), channel_id=1, source_target_pairs={{0,64},{64,128},{128,192},{192,0},{256,320},{320,384},{384,448},{4... | collective-permute-start | bytes 2162696 | tf_op jit(solution)/shard_map/ppermute | solution.py:236
  164.7 1.9 collective-permute-start.2
  166.6 5.1 %collective-permute-start.6 = (bf16[4,64,1664]{2,1,0:T(8,128)(2,1)}, bf16[4,64,1664]{2,1,0:T(8,128)(2,1)S(1)}, u32[]{:S(2)}, u32[]{:S(2)}) collective-permute-start(bf16[4,64,1664]{2,1,0:T(8,128)(2,1)} %get-tuple-element.35), channel_id=1, source_target_pairs={{0,512},{64,576},{128,640},{192,704},{256,768},{320,832},{384,896}... | collective-permute-start | bytes 2555912 | tf_op jit(solution)/shard_map/ppermute | solution.py:236
  171.7 2.6 %collective-permute-start.7 = (bf16[4,64,1664]{2,1,0:T(8,128)(2,1)}, bf16[4,64,1664]{2,1,0:T(8,128)(2,1)S(1)}, u32[]{:S(2)}, u32[]{:S(2)}) collective-permute-start(bf16[4,64,1664]{2,1,0:T(8,128)(2,1)} %get-tuple-element.36), channel_id=1, source_target_pairs={{0,256},{64,320},{128,384},{192,448},{256,512},{320,576},{384,640}... | collective-permute-start | bytes 2555912 | tf_op jit(solution)/shard_map/ppermute | solution.py:236
  174.3 5.7 %collective-permute-done.refs_1_ = bf16[4,64,1408]{2,1,0:T(8,128)(2,1)S(1)} collective-permute-done((bf16[4,64,1408]{2,1,0:T(8,128)(2,1)}, bf16[4,64,1408]{2,1,0:T(8,128)(2,1)S(1)}, u32[]{:S(2)}, u32[]{:S(2)}) %collective-permute-start) | collective-permute-done | bytes 720928 | tf_op jit(solution)/shard_map/ppermute | solution.py:236
  180.0 4.9 %collective-permute-start.8 = (bf16[4,64,1664]{2,1,0:T(8,128)(2,1)}, bf16[4,64,1664]{2,1,0:T(8,128)(2,1)S(1)}, u32[]{:S(2)}, u32[]{:S(2)}) collective-permute-start(bf16[4,64,1664]{2,1,0:T(8,128)(2,1)} %get-tuple-element.37), channel_id=1, source_target_pairs={{0,768},{64,832},{128,896},{192,960},{256,0},{320,64},{384,128},{4... | collective-permute-start | bytes 2555912 | tf_op jit(solution)/shard_map/ppermute | solution.py:236
  184.9 7.3 %collective-permute-done.1.refs_2_ = bf16[4,64,1408]{2,1,0:T(8,128)(2,1)S(1)} collective-permute-done((bf16[4,64,1408]{2,1,0:T(8,128)(2,1)}, bf16[4,64,1408]{2,1,0:T(8,128)(2,1)S(1)}, u32[]{:S(2)}, u32[]{:S(2)}) %collective-permute-start.1) | collective-permute-done | bytes 720928 | tf_op jit(solution)/shard_map/ppermute | solution.py:236
  192.3 2.2 collective-permute-done.2.refs_3_
  194.4 0.0 copy-start.1
  194.4 1.1 copy-done.1
  195.5 0.3 shard_map.87
  195.9 5.1 %collective-permute-start.3 = (bf16[64,1664]{1,0:T(8,128)(2,1)S(1)}, bf16[64,1664]{1,0:T(8,128)(2,1)S(1)}, u32[]{:S(2)}, u32[]{:S(2)}) collective-permute-start(bf16[64,1664]{1,0:T(8,128)(2,1)S(1)} %get-tuple-element.31), channel_id=1, source_target_pairs={{0,512},{64,576},{128,640},{192,704},{256,768},{320,832},{384,896}... | collective-permute-start | bytes 638984 | tf_op jit(solution)/shard_map/ppermute | solution.py:236
  201.0 2.6 %collective-permute-start.4 = (bf16[64,1664]{1,0:T(8,128)(2,1)S(1)}, bf16[64,1664]{1,0:T(8,128)(2,1)S(1)}, u32[]{:S(2)}, u32[]{:S(2)}) collective-permute-start(bf16[64,1664]{1,0:T(8,128)(2,1)S(1)} %get-tuple-element.32), channel_id=1, source_target_pairs={{0,256},{64,320},{128,384},{192,448},{256,512},{320,576},{384,640}... | collective-permute-start | bytes 638984 | tf_op jit(solution)/shard_map/ppermute | solution.py:236
  203.6 0.0 collective-permute-done.6.refs_1_
  203.6 4.5 %collective-permute-start.5 = (bf16[64,1664]{1,0:T(8,128)(2,1)S(1)}, bf16[64,1664]{1,0:T(8,128)(2,1)S(1)}, u32[]{:S(2)}, u32[]{:S(2)}) collective-permute-start(bf16[64,1664]{1,0:T(8,128)(2,1)S(1)} %get-tuple-element.33), channel_id=1, source_target_pairs={{0,768},{64,832},{128,896},{192,960},{256,0},{320,64},{384,128},{4... | collective-permute-start | bytes 638984 | tf_op jit(solution)/shard_map/ppermute | solution.py:236
  208.1 2.4 %collective-permute-done.7.refs_2_ = bf16[4,64,1664]{2,1,0:T(8,128)(2,1)S(1)} collective-permute-done((bf16[4,64,1664]{2,1,0:T(8,128)(2,1)}, bf16[4,64,1664]{2,1,0:T(8,128)(2,1)S(1)}, u32[]{:S(2)}, u32[]{:S(2)}) %collective-permute-start.7) | collective-permute-done | bytes 852000 | tf_op jit(solution)/shard_map/ppermute | solution.py:236
  210.5 0.3 collective-permute-done.8.refs_3_
  210.8 0.0 copy-done
  210.8 0.4 shard_map.88
  211.2 4.0 %collective-permute-start.9 = (bf16[64,1664]{1,0:T(8,128)(2,1)S(1)}, bf16[64,1664]{1,0:T(8,128)(2,1)S(1)}, u32[]{:S(2)}, u32[]{:S(2)}) collective-permute-start(bf16[64,1664]{1,0:T(8,128)(2,1)S(1)} %get-tuple-element.39), channel_id=1, source_target_pairs={{0,128},{64,192},{128,0},{192,64},{256,384},{320,448},{384,256},{4... | collective-permute-start | bytes 638984 | tf_op jit(solution)/shard_map/ppermute | solution.py:236
  215.1 3.1 %collective-permute-start.10 = (bf16[64,1664]{1,0:T(8,128)(2,1)S(1)}, bf16[64,1664]{1,0:T(8,128)(2,1)S(1)}, u32[]{:S(2)}, u32[]{:S(2)}) collective-permute-start(bf16[64,1664]{1,0:T(8,128)(2,1)S(1)} %get-tuple-element.40), channel_id=1, source_target_pairs={{0,64},{64,128},{128,192},{192,0},{256,320},{320,384},{384,448},{4... | collective-permute-start | bytes 638984 | tf_op jit(solution)/shard_map/ppermute | solution.py:236
  218.2 0.0 collective-permute-done.3.refs_1_
  218.3 2.8 %collective-permute-start.11 = (bf16[64,1664]{1,0:T(8,128)(2,1)S(1)}, bf16[64,1664]{1,0:T(8,128)(2,1)S(1)}, u32[]{:S(2)}, u32[]{:S(2)}) collective-permute-start(bf16[64,1664]{1,0:T(8,128)(2,1)S(1)} %get-tuple-element.41), channel_id=1, source_target_pairs={{0,192},{64,0},{128,64},{192,128},{256,448},{320,256},{384,320},{4... | collective-permute-start | bytes 638984 | tf_op jit(solution)/shard_map/ppermute | solution.py:236
  221.0 0.0 collective-permute-done.4.refs_2_
  221.0 0.0 collective-permute-done.5.refs_3_
  221.1 0.2 collective-permute-done.9.refs_5_
  221.2 5.1 %collective-permute-done.10.refs_6_ = bf16[64,1664]{1,0:T(8,128)(2,1)S(1)} collective-permute-done((bf16[64,1664]{1,0:T(8,128)(2,1)S(1)}, bf16[64,1664]{1,0:T(8,128)(2,1)S(1)}, u32[]{:S(2)}, u32[]{:S(2)}) %collective-permute-start.10) | collective-permute-done | bytes 213024 | tf_op jit(solution)/shard_map/ppermute | solution.py:236
  226.3 1.4 collective-permute-done.11.refs_7_
  227.7 0.0 all-to-all-done.1.refs_8_
  227.7 0.0 copy-done.2
  227.7 0.0 copy-done.3
  227.7 1.3 shard_map.89
Async XLA Ops:
  152.6 58.2 %copy-start = (bf16[4,64,1664]{2,1,0:T(8,128)(2,1)S(1)}, bf16[4,64,1664]{2,1,0:T(8,128)(2,1)}, u32[]{:S(2)}) copy-start(bf16[4,64,1664]{2,1,0:T(8,128)(2,1)} %get-tuple-element.34.refs_0_) | copy-start | bytes 2555908
  152.6 75.2 %copy-start.2 = (f32[128,1]{0,1:T(1,128)S(1)}, f32[128,1]{0,1:T(1,128)}, u32[]{:S(2)}) copy-start(f32[128,1]{0,1:T(1,128)} %param.9) | copy-start | bytes 1540
  152.6 75.2 %copy-start.3 = (s32[1,128]{1,0:T(1,128)S(1)}, s32[1,128]{1,0:T(1,128)}, u32[]{:S(2)}) copy-start(s32[1,128]{1,0:T(1,128)} %get-tuple-element.43.refs_9_) | copy-start | bytes 1540
  152.6 75.1 %all-to-all-start.1 = ((bf16[64,4,1024]{2,1,0:T(4,128)(2,1)}), bf16[64,4,1024]{2,1,0:T(4,128)(2,1)S(1)}, u32[]{:S(2)}, u32[]{:S(2)}) async-start(bf16[64,4,1024]{2,1,0:T(4,128)(2,1)} %get-tuple-element.42), calls=%async_computation.1 | async-start | bytes 1048576 | tf_op jit(solution)/shard_map/all_to_all | solution.py:229
  157.4 22.7 %collective-permute-start = (bf16[4,64,1408]{2,1,0:T(8,128)(2,1)}, bf16[4,64,1408]{2,1,0:T(8,128)(2,1)S(1)}, u32[]{:S(2)}, u32[]{:S(2)}) collective-permute-start(bf16[4,64,1408]{2,1,0:T(8,128)(2,1)} %get-tuple-element.27), channel_id=1, source_target_pairs={{0,128},{64,192},{128,0},{192,64},{256,384},{320,448},{384,256},{4... | collective-permute-start | bytes 2162696 | tf_op jit(solution)/shard_map/ppermute | solution.py:236
  160.7 31.6 %collective-permute-start.1 = (bf16[4,64,1408]{2,1,0:T(8,128)(2,1)}, bf16[4,64,1408]{2,1,0:T(8,128)(2,1)S(1)}, u32[]{:S(2)}, u32[]{:S(2)}) collective-permute-start(bf16[4,64,1408]{2,1,0:T(8,128)(2,1)} %get-tuple-element.28), channel_id=1, source_target_pairs={{0,64},{64,128},{128,192},{192,0},{256,320},{320,384},{384,448},{4... | collective-permute-start | bytes 2162696 | tf_op jit(solution)/shard_map/ppermute | solution.py:236
  164.7 29.7 %collective-permute-start.2 = (bf16[4,64,1408]{2,1,0:T(8,128)(2,1)}, bf16[4,64,1408]{2,1,0:T(8,128)(2,1)S(1)}, u32[]{:S(2)}, u32[]{:S(2)}) collective-permute-start(bf16[4,64,1408]{2,1,0:T(8,128)(2,1)} %get-tuple-element.29), channel_id=1, source_target_pairs={{0,192},{64,0},{128,64},{192,128},{256,448},{320,256},{384,320},{4... | collective-permute-start | bytes 2162696 | tf_op jit(solution)/shard_map/ppermute | solution.py:236
  166.6 37.0 %collective-permute-start.6 = (bf16[4,64,1664]{2,1,0:T(8,128)(2,1)}, bf16[4,64,1664]{2,1,0:T(8,128)(2,1)S(1)}, u32[]{:S(2)}, u32[]{:S(2)}) collective-permute-start(bf16[4,64,1664]{2,1,0:T(8,128)(2,1)} %get-tuple-element.35), channel_id=1, source_target_pairs={{0,512},{64,576},{128,640},{192,704},{256,768},{320,832},{384,896}... | collective-permute-start | bytes 2555912 | tf_op jit(solution)/shard_map/ppermute | solution.py:236
  171.7 38.7 %collective-permute-start.7 = (bf16[4,64,1664]{2,1,0:T(8,128)(2,1)}, bf16[4,64,1664]{2,1,0:T(8,128)(2,1)S(1)}, u32[]{:S(2)}, u32[]{:S(2)}) collective-permute-start(bf16[4,64,1664]{2,1,0:T(8,128)(2,1)} %get-tuple-element.36), channel_id=1, source_target_pairs={{0,256},{64,320},{128,384},{192,448},{256,512},{320,576},{384,640}... | collective-permute-start | bytes 2555912 | tf_op jit(solution)/shard_map/ppermute | solution.py:236
  180.0 30.7 %collective-permute-start.8 = (bf16[4,64,1664]{2,1,0:T(8,128)(2,1)}, bf16[4,64,1664]{2,1,0:T(8,128)(2,1)S(1)}, u32[]{:S(2)}, u32[]{:S(2)}) collective-permute-start(bf16[4,64,1664]{2,1,0:T(8,128)(2,1)} %get-tuple-element.37), channel_id=1, source_target_pairs={{0,768},{64,832},{128,896},{192,960},{256,0},{320,64},{384,128},{4... | collective-permute-start | bytes 2555912 | tf_op jit(solution)/shard_map/ppermute | solution.py:236
  194.4 1.1 copy-start.1
  195.9 22.4 %collective-permute-start.3 = (bf16[64,1664]{1,0:T(8,128)(2,1)S(1)}, bf16[64,1664]{1,0:T(8,128)(2,1)S(1)}, u32[]{:S(2)}, u32[]{:S(2)}) collective-permute-start(bf16[64,1664]{1,0:T(8,128)(2,1)S(1)} %get-tuple-element.31), channel_id=1, source_target_pairs={{0,512},{64,576},{128,640},{192,704},{256,768},{320,832},{384,896}... | collective-permute-start | bytes 638984 | tf_op jit(solution)/shard_map/ppermute | solution.py:236
  201.0 20.1 %collective-permute-start.4 = (bf16[64,1664]{1,0:T(8,128)(2,1)S(1)}, bf16[64,1664]{1,0:T(8,128)(2,1)S(1)}, u32[]{:S(2)}, u32[]{:S(2)}) collective-permute-start(bf16[64,1664]{1,0:T(8,128)(2,1)S(1)} %get-tuple-element.32), channel_id=1, source_target_pairs={{0,256},{64,320},{128,384},{192,448},{256,512},{320,576},{384,640}... | collective-permute-start | bytes 638984 | tf_op jit(solution)/shard_map/ppermute | solution.py:236
  203.6 17.5 %collective-permute-start.5 = (bf16[64,1664]{1,0:T(8,128)(2,1)S(1)}, bf16[64,1664]{1,0:T(8,128)(2,1)S(1)}, u32[]{:S(2)}, u32[]{:S(2)}) collective-permute-start(bf16[64,1664]{1,0:T(8,128)(2,1)S(1)} %get-tuple-element.33), channel_id=1, source_target_pairs={{0,768},{64,832},{128,896},{192,960},{256,0},{320,64},{384,128},{4... | collective-permute-start | bytes 638984 | tf_op jit(solution)/shard_map/ppermute | solution.py:236
  211.2 10.0 %collective-permute-start.9 = (bf16[64,1664]{1,0:T(8,128)(2,1)S(1)}, bf16[64,1664]{1,0:T(8,128)(2,1)S(1)}, u32[]{:S(2)}, u32[]{:S(2)}) collective-permute-start(bf16[64,1664]{1,0:T(8,128)(2,1)S(1)} %get-tuple-element.39), channel_id=1, source_target_pairs={{0,128},{64,192},{128,0},{192,64},{256,384},{320,448},{384,256},{4... | collective-permute-start | bytes 638984 | tf_op jit(solution)/shard_map/ppermute | solution.py:236
  215.1 11.2 %collective-permute-start.10 = (bf16[64,1664]{1,0:T(8,128)(2,1)S(1)}, bf16[64,1664]{1,0:T(8,128)(2,1)S(1)}, u32[]{:S(2)}, u32[]{:S(2)}) collective-permute-start(bf16[64,1664]{1,0:T(8,128)(2,1)S(1)} %get-tuple-element.40), channel_id=1, source_target_pairs={{0,64},{64,128},{128,192},{192,0},{256,320},{320,384},{384,448},{4... | collective-permute-start | bytes 638984 | tf_op jit(solution)/shard_map/ppermute | solution.py:236
  218.3 9.5 %collective-permute-start.11 = (bf16[64,1664]{1,0:T(8,128)(2,1)S(1)}, bf16[64,1664]{1,0:T(8,128)(2,1)S(1)}, u32[]{:S(2)}, u32[]{:S(2)}) collective-permute-start(bf16[64,1664]{1,0:T(8,128)(2,1)S(1)} %get-tuple-element.41), channel_id=1, source_target_pairs={{0,192},{64,0},{128,64},{192,128},{256,448},{320,256},{384,320},{4... | collective-permute-start | bytes 638984 | tf_op jit(solution)/shard_map/ppermute | solution.py:236

commit v5 on v4

--- a/solution.py
+++ b/solution.py
@@ -70,8 +70,7 @@
 
 
 def half_columns(hidden):
-    few = 3 * hidden // 8
-    return few, hidden - few
+    return hidden // 2, hidden // 2
 
 
 def expert_kernel(cap, wi_hbm, wo_hbm, got_hbm, y_hbm, *refs):
@@ -153,10 +152,7 @@
         total = parts[0][at].astype(F32)
         for part in parts[1:]:
             total = total + part[at].astype(F32)
-        cols = total.shape[1]
-        outs[t][:, :cols] = total.astype(outs[t].dtype)
-        if cols < outs[t].shape[1]:
-            outs[t][:, cols:] = jnp.zeros((total.shape[0], outs[t].shape[1] - cols), outs[t].dtype)
+        outs[t][...] = total.astype(outs[t].dtype)
 
 
 def last_kernel(*refs):
@@ -241,13 +237,13 @@
         b[k] = shift(b[k], k, 0)
     ends = []
     for axis, half in enumerate((a, b)):
-        c = max(cols)
+        c = cols[axis]
         mids = call(
             functools.partial(middle_kernel, axis),
             [((share, c), F32)] + [((share, c), BF)] * (RING - 1),
             8 * MIB, 5 * MIB, RING,
-        )(half[0], half[2], half[1], half[3])
-        far = [shift(mids[t], t, 0) if axis == 0 else shift(mids[t], 0, t) for t in (2, 1, 3)]
+        )(half[0], *[half[k] for k in ((2, 1, 3), (1, 3, 2))[axis]])
+        far = [shift(mids[t], t, 0) if axis == 0 else shift(mids[t], 0, t) for t in ((1, 3, 2), (2, 1, 3))[axis]]
         ends += [mids[0]] + far
     output, grad_in, grad_out = call(
         last_kernel,

time: 232 us -> 229 us (0.987)
  transfers between devices with their start and end apart: 13 -> 13, of which waited for: 8 -> 6; matrix products, arithmetic and copies ran while one was open for 0% -> 0% of each run, Pallas kernels for 0% -> 0%
where the time goes in v5:
time: 229 us; the launch traced here: 227 us
  blocking collectives  140 us (61%)
  starting transfers between devices  46.3 us (20%)
  waiting for transfers between devices  25.3 us (11%)
  Pallas kernels  13.7 us (6%)
    all_to_all x1, blocking collectives, on_device(): lax.all_to_all(send.reshape(n_experts, 2 * cap, width), 'expert', split_a...  140 us
    ppermute x12, starting transfers between devices, shift(): return lax.ppermute(v, 'dp', pairs)  41.6 us
    ppermute x12, waiting for transfers between devices, shift(): return lax.ppermute(v, 'dp', pairs)  25.3 us
    pallas_call x1, Pallas kernels, on_device(): call(functools.partial(expert_kernel, cap), [((n_experts, cap, width), BF...  8.98 us
    all_to_all x1, starting transfers between devices, on_device(): lax.all_to_all(y_buf, 'expert', split_axis=0, concat_axis=0, tiled=True)  4.78 us
  transfers between devices with their start and end apart: 13, of which 6 were waited for; matrix products, arithmetic and copies ran while one was open for 0% of the time, Pallas kernels for 0%

profile of v5, /device:TPU:6, one launch (start us, length us, event | category | flops | bytes accessed | tf_op | source)
XLA Modules:
  0.0 227.5 jit_solution(14032182248773283827)
XLA Ops:
  0.6 2.7 %shard_map.85 = (bf16[512,1024]{1,0:T(8,128)(2,1)}, s32[1,128]{1,0:T(1,128)}) custom-call(bf16[128,1024]{1,0:T(8,128)(2,1)} %x_hbm.1, bf16[128,1024]{1,0:T(8,128)(2,1)} %c_hbm.1, s32[1,128]{1,0:T(1,128)} %bitcast.16, f32[1,128]{1,0:T(1,128)} %bitcast.8), custom_call_target="tpu_custom_call" | custom-call | flops 268435456 | bytes 4194304 | tf_op jit(solution)/shard_map/pallas_call | solution.py:188
  3.3 140.2 %all_to_all.10 = bf16[64,8,1024]{2,1,0:T(8,128)(2,1)} all-to-all(bf16[64,8,1024]{2,1,0:T(8,128)(2,1)} %bitcast.11), channel_id=1, replica_groups=mesh['dp'=16,'expert'=64] {'expert'}, dimensions={0} | all-to-all | bytes 2097152 | tf_op jit(solution)/shard_map/all_to_all | solution.py:200
  143.5 9.0 %shard_map.86 = (bf16[64,4,1024]{2,1,0:T(4,128)(2,1)}, bf16[4,64,1536]{2,1,0:T(8,128)(2,1)}, bf16[4,64,1536]{2,1,0:T(8,128)(2,1)}, bf16[4,64,1536]{2,1,0:T(8,128...) custom-call(bf16[1024,2048]{1,0:T(8,128)(2,1)} %bitcast.12, ...), custom_call_target="tpu_custom_call" | custom-call | flops 4294967296 | bytes 16777216 | tf_op jit(solution)/shard_map/pallas_call | solution.py:206
  152.5 0.0 copy-start
  152.5 0.0 copy-start.2
  152.5 0.0 copy-start.3
  152.5 4.8 %all-to-all-start.1 = ((bf16[64,4,1024]{2,1,0:T(4,128)(2,1)}), bf16[64,4,1024]{2,1,0:T(4,128)(2,1)S(1)}, u32[]{:S(2)}, u32[]{:S(2)}) async-start(bf16[64,4,1024]{2,1,0:T(4,128)(2,1)} %get-tuple-element.42), calls=%async_computation.1 | async-start | bytes 1048576 | tf_op jit(solution)/shard_map/all_to_all | solution.py:225
  157.3 3.3 %collective-permute-start = (bf16[4,64,1536]{2,1,0:T(8,128)(2,1)}, bf16[4,64,1536]{2,1,0:T(8,128)(2,1)S(1)}, u32[]{:S(2)}, u32[]{:S(2)}) collective-permute-start(bf16[4,64,1536]{2,1,0:T(8,128)(2,1)} %get-tuple-element.27), channel_id=1, source_target_pairs={{0,128},{64,192},{128,0},{192,64},{256,384},{320,448},{384,256},{4... | collective-permute-start | bytes 2359304 | tf_op jit(solution)/shard_map/ppermute | solution.py:232
  160.6 4.0 %collective-permute-start.1 = (bf16[4,64,1536]{2,1,0:T(8,128)(2,1)}, bf16[4,64,1536]{2,1,0:T(8,128)(2,1)S(1)}, u32[]{:S(2)}, u32[]{:S(2)}) collective-permute-start(bf16[4,64,1536]{2,1,0:T(8,128)(2,1)} %get-tuple-element.28), channel_id=1, source_target_pairs={{0,64},{64,128},{128,192},{192,0},{256,320},{320,384},{384,448},{4... | collective-permute-start | bytes 2359304 | tf_op jit(solution)/shard_map/ppermute | solution.py:232
  164.6 1.9 collective-permute-start.2
  166.5 3.5 %collective-permute-start.6 = (bf16[4,64,1536]{2,1,0:T(8,128)(2,1)}, bf16[4,64,1536]{2,1,0:T(8,128)(2,1)S(1)}, u32[]{:S(2)}, u32[]{:S(2)}) collective-permute-start(bf16[4,64,1536]{2,1,0:T(8,128)(2,1)} %get-tuple-element.35), channel_id=1, source_target_pairs={{0,256},{64,320},{128,384},{192,448},{256,512},{320,576},{384,640}... | collective-permute-start | bytes 2359304 | tf_op jit(solution)/shard_map/ppermute | solution.py:232
  170.0 3.6 %collective-permute-start.7 = (bf16[4,64,1536]{2,1,0:T(8,128)(2,1)}, bf16[4,64,1536]{2,1,0:T(8,128)(2,1)S(1)}, u32[]{:S(2)}, u32[]{:S(2)}) collective-permute-start(bf16[4,64,1536]{2,1,0:T(8,128)(2,1)} %get-tuple-element.36), channel_id=1, source_target_pairs={{0,768},{64,832},{128,896},{192,960},{256,0},{320,64},{384,128},{4... | collective-permute-start | bytes 2359304 | tf_op jit(solution)/shard_map/ppermute | solution.py:232
  173.6 7.7 %collective-permute-done.refs_1_ = bf16[4,64,1536]{2,1,0:T(8,128)(2,1)S(1)} collective-permute-done((bf16[4,64,1536]{2,1,0:T(8,128)(2,1)}, bf16[4,64,1536]{2,1,0:T(8,128)(2,1)S(1)}, u32[]{:S(2)}, u32[]{:S(2)}) %collective-permute-start) | collective-permute-done | bytes 786464 | tf_op jit(solution)/shard_map/ppermute | solution.py:232
  181.4 5.1 %collective-permute-start.8 = (bf16[4,64,1536]{2,1,0:T(8,128)(2,1)}, bf16[4,64,1536]{2,1,0:T(8,128)(2,1)S(1)}, u32[]{:S(2)}, u32[]{:S(2)}) collective-permute-start(bf16[4,64,1536]{2,1,0:T(8,128)(2,1)} %get-tuple-element.37), channel_id=1, source_target_pairs={{0,512},{64,576},{128,640},{192,704},{256,768},{320,832},{384,896}... | collective-permute-start | bytes 2359304 | tf_op jit(solution)/shard_map/ppermute | solution.py:232
  186.5 8.5 %collective-permute-done.1.refs_2_ = bf16[4,64,1536]{2,1,0:T(8,128)(2,1)S(1)} collective-permute-done((bf16[4,64,1536]{2,1,0:T(8,128)(2,1)}, bf16[4,64,1536]{2,1,0:T(8,128)(2,1)S(1)}, u32[]{:S(2)}, u32[]{:S(2)}) %collective-permute-start.1) | collective-permute-done | bytes 786464 | tf_op jit(solution)/shard_map/ppermute | solution.py:232
  195.0 2.2 collective-permute-done.2.refs_3_
  197.1 0.0 copy-start.1
  197.1 1.1 copy-done.1
  198.3 0.4 shard_map.87
  198.7 3.5 %collective-permute-start.3 = (bf16[64,1536]{1,0:T(8,128)(2,1)S(1)}, bf16[64,1536]{1,0:T(8,128)(2,1)S(1)}, u32[]{:S(2)}, u32[]{:S(2)}) collective-permute-start(bf16[64,1536]{1,0:T(8,128)(2,1)S(1)} %get-tuple-element.31), channel_id=1, source_target_pairs={{0,256},{64,320},{128,384},{192,448},{256,512},{320,576},{384,640}... | collective-permute-start | bytes 589832 | tf_op jit(solution)/shard_map/ppermute | solution.py:232
  202.2 3.6 %collective-permute-start.4 = (bf16[64,1536]{1,0:T(8,128)(2,1)S(1)}, bf16[64,1536]{1,0:T(8,128)(2,1)S(1)}, u32[]{:S(2)}, u32[]{:S(2)}) collective-permute-start(bf16[64,1536]{1,0:T(8,128)(2,1)S(1)} %get-tuple-element.32), channel_id=1, source_target_pairs={{0,768},{64,832},{128,896},{192,960},{256,0},{320,64},{384,128},{4... | collective-permute-start | bytes 589832 | tf_op jit(solution)/shard_map/ppermute | solution.py:232
  205.7 0.0 collective-permute-done.6.refs_1_
  205.7 3.9 %collective-permute-start.5 = (bf16[64,1536]{1,0:T(8,128)(2,1)S(1)}, bf16[64,1536]{1,0:T(8,128)(2,1)S(1)}, u32[]{:S(2)}, u32[]{:S(2)}) collective-permute-start(bf16[64,1536]{1,0:T(8,128)(2,1)S(1)} %get-tuple-element.33), channel_id=1, source_target_pairs={{0,512},{64,576},{128,640},{192,704},{256,768},{320,832},{384,896}... | collective-permute-start | bytes 589832 | tf_op jit(solution)/shard_map/ppermute | solution.py:232
  209.6 0.0 collective-permute-done.7.refs_2_
  209.7 0.0 collective-permute-done.8.refs_3_
  209.7 0.0 copy-done
  209.7 0.4 shard_map.88
  210.1 3.4 %collective-permute-start.9 = (bf16[64,1536]{1,0:T(8,128)(2,1)S(1)}, bf16[64,1536]{1,0:T(8,128)(2,1)S(1)}, u32[]{:S(2)}, u32[]{:S(2)}) collective-permute-start(bf16[64,1536]{1,0:T(8,128)(2,1)S(1)} %get-tuple-element.39), channel_id=1, source_target_pairs={{0,128},{64,192},{128,0},{192,64},{256,384},{320,448},{384,256},{4... | collective-permute-start | bytes 589832 | tf_op jit(solution)/shard_map/ppermute | solution.py:232
  213.5 3.9 %collective-permute-start.10 = (bf16[64,1536]{1,0:T(8,128)(2,1)S(1)}, bf16[64,1536]{1,0:T(8,128)(2,1)S(1)}, u32[]{:S(2)}, u32[]{:S(2)}) collective-permute-start(bf16[64,1536]{1,0:T(8,128)(2,1)S(1)} %get-tuple-element.40), channel_id=1, source_target_pairs={{0,64},{64,128},{128,192},{192,0},{256,320},{320,384},{384,448},{4... | collective-permute-start | bytes 589832 | tf_op jit(solution)/shard_map/ppermute | solution.py:232
  217.4 0.0 collective-permute-done.3.refs_1_
  217.4 1.9 collective-permute-start.11
  219.3 0.0 collective-permute-done.4.refs_2_
  219.4 0.0 collective-permute-done.5.refs_3_
  219.4 0.1 collective-permute-done.9.refs_5_
  219.5 3.2 %collective-permute-done.10.refs_6_ = bf16[64,1536]{1,0:T(8,128)(2,1)S(1)} collective-permute-done((bf16[64,1536]{1,0:T(8,128)(2,1)S(1)}, bf16[64,1536]{1,0:T(8,128)(2,1)S(1)}, u32[]{:S(2)}, u32[]{:S(2)}) %collective-permute-start.10) | collective-permute-done | bytes 196640 | tf_op jit(solution)/shard_map/ppermute | solution.py:232
  222.7 3.5 %collective-permute-done.11.refs_7_ = bf16[64,1536]{1,0:T(8,128)(2,1)S(1)} collective-permute-done((bf16[64,1536]{1,0:T(8,128)(2,1)S(1)}, bf16[64,1536]{1,0:T(8,128)(2,1)S(1)}, u32[]{:S(2)}, u32[]{:S(2)}) %collective-permute-start.11) | collective-permute-done | bytes 196640 | tf_op jit(solution)/shard_map/ppermute | solution.py:232
  226.2 0.0 all-to-all-done.1.refs_8_
  226.2 0.0 copy-done.2
  226.2 0.0 copy-done.3
  226.2 1.2 shard_map.89
Async XLA Ops:
  152.5 57.2 %copy-start = (bf16[4,64,1536]{2,1,0:T(8,128)(2,1)S(1)}, bf16[4,64,1536]{2,1,0:T(8,128)(2,1)}, u32[]{:S(2)}) copy-start(bf16[4,64,1536]{2,1,0:T(8,128)(2,1)} %get-tuple-element.34.refs_0_) | copy-start | bytes 2359300
  152.5 73.7 %copy-start.2 = (f32[128,1]{0,1:T(1,128)S(1)}, f32[128,1]{0,1:T(1,128)}, u32[]{:S(2)}) copy-start(f32[128,1]{0,1:T(1,128)} %param.9) | copy-start | bytes 1540
  152.5 73.7 %copy-start.3 = (s32[1,128]{1,0:T(1,128)S(1)}, s32[1,128]{1,0:T(1,128)}, u32[]{:S(2)}) copy-start(s32[1,128]{1,0:T(1,128)} %get-tuple-element.43.refs_9_) | copy-start | bytes 1540
  152.5 73.7 %all-to-all-start.1 = ((bf16[64,4,1024]{2,1,0:T(4,128)(2,1)}), bf16[64,4,1024]{2,1,0:T(4,128)(2,1)S(1)}, u32[]{:S(2)}, u32[]{:S(2)}) async-start(bf16[64,4,1024]{2,1,0:T(4,128)(2,1)} %get-tuple-element.42), calls=%async_computation.1 | async-start | bytes 1048576 | tf_op jit(solution)/shard_map/all_to_all | solution.py:225
  157.3 24.1 %collective-permute-start = (bf16[4,64,1536]{2,1,0:T(8,128)(2,1)}, bf16[4,64,1536]{2,1,0:T(8,128)(2,1)S(1)}, u32[]{:S(2)}, u32[]{:S(2)}) collective-permute-start(bf16[4,64,1536]{2,1,0:T(8,128)(2,1)} %get-tuple-element.27), channel_id=1, source_target_pairs={{0,128},{64,192},{128,0},{192,64},{256,384},{320,448},{384,256},{4... | collective-permute-start | bytes 2359304 | tf_op jit(solution)/shard_map/ppermute | solution.py:232
  160.6 34.4 %collective-permute-start.1 = (bf16[4,64,1536]{2,1,0:T(8,128)(2,1)}, bf16[4,64,1536]{2,1,0:T(8,128)(2,1)S(1)}, u32[]{:S(2)}, u32[]{:S(2)}) collective-permute-start(bf16[4,64,1536]{2,1,0:T(8,128)(2,1)} %get-tuple-element.28), channel_id=1, source_target_pairs={{0,64},{64,128},{128,192},{192,0},{256,320},{320,384},{384,448},{4... | collective-permute-start | bytes 2359304 | tf_op jit(solution)/shard_map/ppermute | solution.py:232
  164.6 32.5 %collective-permute-start.2 = (bf16[4,64,1536]{2,1,0:T(8,128)(2,1)}, bf16[4,64,1536]{2,1,0:T(8,128)(2,1)S(1)}, u32[]{:S(2)}, u32[]{:S(2)}) collective-permute-start(bf16[4,64,1536]{2,1,0:T(8,128)(2,1)} %get-tuple-element.29), channel_id=1, source_target_pairs={{0,192},{64,0},{128,64},{192,128},{256,448},{320,256},{384,320},{4... | collective-permute-start | bytes 2359304 | tf_op jit(solution)/shard_map/ppermute | solution.py:232
  166.5 39.2 %collective-permute-start.6 = (bf16[4,64,1536]{2,1,0:T(8,128)(2,1)}, bf16[4,64,1536]{2,1,0:T(8,128)(2,1)S(1)}, u32[]{:S(2)}, u32[]{:S(2)}) collective-permute-start(bf16[4,64,1536]{2,1,0:T(8,128)(2,1)} %get-tuple-element.35), channel_id=1, source_target_pairs={{0,256},{64,320},{128,384},{192,448},{256,512},{320,576},{384,640}... | collective-permute-start | bytes 2359304 | tf_op jit(solution)/shard_map/ppermute | solution.py:232
  170.0 39.6 %collective-permute-start.7 = (bf16[4,64,1536]{2,1,0:T(8,128)(2,1)}, bf16[4,64,1536]{2,1,0:T(8,128)(2,1)S(1)}, u32[]{:S(2)}, u32[]{:S(2)}) collective-permute-start(bf16[4,64,1536]{2,1,0:T(8,128)(2,1)} %get-tuple-element.36), channel_id=1, source_target_pairs={{0,768},{64,832},{128,896},{192,960},{256,0},{320,64},{384,128},{4... | collective-permute-start | bytes 2359304 | tf_op jit(solution)/shard_map/ppermute | solution.py:232
  181.4 28.3 %collective-permute-start.8 = (bf16[4,64,1536]{2,1,0:T(8,128)(2,1)}, bf16[4,64,1536]{2,1,0:T(8,128)(2,1)S(1)}, u32[]{:S(2)}, u32[]{:S(2)}) collective-permute-start(bf16[4,64,1536]{2,1,0:T(8,128)(2,1)} %get-tuple-element.37), channel_id=1, source_target_pairs={{0,512},{64,576},{128,640},{192,704},{256,768},{320,832},{384,896}... | collective-permute-start | bytes 2359304 | tf_op jit(solution)/shard_map/ppermute | solution.py:232
  197.1 1.1 copy-start.1
  198.7 18.8 %collective-permute-start.3 = (bf16[64,1536]{1,0:T(8,128)(2,1)S(1)}, bf16[64,1536]{1,0:T(8,128)(2,1)S(1)}, u32[]{:S(2)}, u32[]{:S(2)}) collective-permute-start(bf16[64,1536]{1,0:T(8,128)(2,1)S(1)} %get-tuple-element.31), channel_id=1, source_target_pairs={{0,256},{64,320},{128,384},{192,448},{256,512},{320,576},{384,640}... | collective-permute-start | bytes 589832 | tf_op jit(solution)/shard_map/ppermute | solution.py:232
  202.2 17.2 %collective-permute-start.4 = (bf16[64,1536]{1,0:T(8,128)(2,1)S(1)}, bf16[64,1536]{1,0:T(8,128)(2,1)S(1)}, u32[]{:S(2)}, u32[]{:S(2)}) collective-permute-start(bf16[64,1536]{1,0:T(8,128)(2,1)S(1)} %get-tuple-element.32), channel_id=1, source_target_pairs={{0,768},{64,832},{128,896},{192,960},{256,0},{320,64},{384,128},{4... | collective-permute-start | bytes 589832 | tf_op jit(solution)/shard_map/ppermute | solution.py:232
  205.7 13.6 %collective-permute-start.5 = (bf16[64,1536]{1,0:T(8,128)(2,1)S(1)}, bf16[64,1536]{1,0:T(8,128)(2,1)S(1)}, u32[]{:S(2)}, u32[]{:S(2)}) collective-permute-start(bf16[64,1536]{1,0:T(8,128)(2,1)S(1)} %get-tuple-element.33), channel_id=1, source_target_pairs={{0,512},{64,576},{128,640},{192,704},{256,768},{320,832},{384,896}... | collective-permute-start | bytes 589832 | tf_op jit(solution)/shard_map/ppermute | solution.py:232
  210.1 9.4 %collective-permute-start.9 = (bf16[64,1536]{1,0:T(8,128)(2,1)S(1)}, bf16[64,1536]{1,0:T(8,128)(2,1)S(1)}, u32[]{:S(2)}, u32[]{:S(2)}) collective-permute-start(bf16[64,1536]{1,0:T(8,128)(2,1)S(1)} %get-tuple-element.39), channel_id=1, source_target_pairs={{0,128},{64,192},{128,0},{192,64},{256,384},{320,448},{384,256},{4... | collective-permute-start | bytes 589832 | tf_op jit(solution)/shard_map/ppermute | solution.py:232
  213.5 9.2 %collective-permute-start.10 = (bf16[64,1536]{1,0:T(8,128)(2,1)S(1)}, bf16[64,1536]{1,0:T(8,128)(2,1)S(1)}, u32[]{:S(2)}, u32[]{:S(2)}) collective-permute-start(bf16[64,1536]{1,0:T(8,128)(2,1)S(1)} %get-tuple-element.40), channel_id=1, source_target_pairs={{0,64},{64,128},{128,192},{192,0},{256,320},{320,384},{384,448},{4... | collective-permute-start | bytes 589832 | tf_op jit(solution)/shard_map/ppermute | solution.py:232
  217.4 8.8 %collective-permute-start.11 = (bf16[64,1536]{1,0:T(8,128)(2,1)S(1)}, bf16[64,1536]{1,0:T(8,128)(2,1)S(1)}, u32[]{:S(2)}, u32[]{:S(2)}) collective-permute-start(bf16[64,1536]{1,0:T(8,128)(2,1)S(1)} %get-tuple-element.41), channel_id=1, source_target_pairs={{0,192},{64,0},{128,64},{192,128},{256,448},{320,256},{384,320},{4... | collective-permute-start | bytes 589832 | tf_op jit(solution)/shard_map/ppermute | solution.py:232

commit v6 on v5

--- a/solution.py
+++ b/solution.py
@@ -35,7 +35,7 @@
     copies = [pltpu.make_async_copy(a, b, sems.at[i]) for i, (a, b) in enumerate(pairs)]
     for copy in copies:
         copy.start()
-    for copy in copies:
+    for copy in copies[:2]:
         copy.wait()
     tok = x_ref.shape[0]
     r = jnp.broadcast_to(r_ref[...], (tok, tok))
@@ -50,6 +50,8 @@
     at = jnp.concatenate([at, at + cap], axis=1)
     rows = lax.broadcasted_iota(jnp.int32, (send_ref.shape[0], 2 * tok), 0)
     placing = jnp.where(rows == at, 1.0, 0.0).astype(BF)
+    for copy in copies[2:]:
+        copy.wait()
     dy = (g * c_ref[...].astype(F32)).astype(BF)
     both = jnp.concatenate([x_ref[...], dy], axis=0)
     send_ref[...] = dot(placing, both, ((1,), (0,))).astype(BF)
@@ -85,13 +87,15 @@
     r = lax.broadcasted_iota(jnp.int32, (n, 1), 0)
     c = lax.broadcasted_iota(jnp.int32, (n, 2 * n), 1)
     at = (r // cap) * (2 * cap) + r % cap
+    pick_x = jnp.where(c == at, 1.0, 0.0).astype(BF)
+    pick_dy = jnp.where(c == at + cap, 1.0, 0.0).astype(BF)
     arrival.wait()
     last.start()
     for copy in copies[2:]:
         copy.start()
     got = got_ref[...]
-    x = dot(jnp.where(c == at, 1.0, 0.0).astype(BF), got, ((1,), (0,))).astype(BF)
-    dy = dot(jnp.where(c == at + cap, 1.0, 0.0).astype(BF), got, ((1,), (0,))).astype(BF)
+    x = dot(pick_x, got, ((1,), (0,))).astype(BF)
+    dy = dot(pick_dy, got, ((1,), (0,))).astype(BF)
     for h in range(0, hidden, STEP):
         copies[2 * h // STEP].wait()
         g = dot(x, wi_ref[:, h : h + STEP], ((1,), (0,)))
@@ -243,7 +247,7 @@
             [((share, c), F32)] + [((share, c), BF)] * (RING - 1),
             8 * MIB, 5 * MIB, RING,
         )(half[0], *[half[k] for k in ((2, 1, 3), (1, 3, 2))[axis]])
-        far = [shift(mids[t], t, 0) if axis == 0 else shift(mids[t], 0, t) for t in ((1, 3, 2), (2, 1, 3))[axis]]
+        far = [shift(mids[t], t, 0) if axis == 0 else shift(mids[t], 0, t) for t in ((3, 1, 2), (2, 1, 3))[axis]]
         ends += [mids[0]] + far
     output, grad_in, grad_out = call(
         last_kernel,

time: 229 us -> 229 us (level)
  transfers between devices with their start and end apart: 13 -> 13, of which waited for: 6 -> 5; matrix products, arithmetic and copies ran while one was open for 0% -> 0% of each run, Pallas kernels for 0% -> 0%
where the time goes in v6:
time: 229 us; the launch traced here: 227 us
  blocking collectives  140 us (61%)
  starting transfers between devices  46.4 us (20%)
  waiting for transfers between devices  25.2 us (11%)
  Pallas kernels  13.6 us (6%)
    all_to_all x1, blocking collectives, on_device(): lax.all_to_all(send.reshape(n_experts, 2 * cap, width), 'expert', split_a...  140 us
    ppermute x12, starting transfers between devices, shift(): return lax.ppermute(v, 'dp', pairs)  41.6 us
    ppermute x12, waiting for transfers between devices, shift(): return lax.ppermute(v, 'dp', pairs)  25.2 us
    pallas_call x1, Pallas kernels, on_device(): call(functools.partial(expert_kernel, cap), [((n_experts, cap, width), BF...  8.98 us
    all_to_all x1, starting transfers between devices, on_device(): lax.all_to_all(y_buf, 'expert', split_axis=0, concat_axis=0, tiled=True)  4.78 us
  transfers between devices with their start and end apart: 13, of which 5 were waited for; matrix products, arithmetic and copies ran while one was open for 0% of the time, Pallas kernels for 0%

profile of v6, /device:TPU:6, one launch (start us, length us, event | category | flops | bytes accessed | tf_op | source)
XLA Modules:
  0.0 227.3 jit_solution(5260976149574012546)
XLA Ops:
  0.6 2.6 %shard_map.85 = (bf16[512,1024]{1,0:T(8,128)(2,1)}, s32[1,128]{1,0:T(1,128)}) custom-call(bf16[128,1024]{1,0:T(8,128)(2,1)} %x_hbm.1, bf16[128,1024]{1,0:T(8,128)(2,1)} %c_hbm.1, s32[1,128]{1,0:T(1,128)} %bitcast.16, f32[1,128]{1,0:T(1,128)} %bitcast.8), custom_call_target="tpu_custom_call" | custom-call | flops 268435456 | bytes 4194304 | tf_op jit(solution)/shard_map/pallas_call | solution.py:192
  3.2 140.2 %all_to_all.10 = bf16[64,8,1024]{2,1,0:T(8,128)(2,1)} all-to-all(bf16[64,8,1024]{2,1,0:T(8,128)(2,1)} %bitcast.11), channel_id=1, replica_groups=mesh['dp'=16,'expert'=64] {'expert'}, dimensions={0} | all-to-all | bytes 2097152 | tf_op jit(solution)/shard_map/all_to_all | solution.py:204
  143.4 9.0 %shard_map.86 = (bf16[64,4,1024]{2,1,0:T(4,128)(2,1)}, bf16[4,64,1536]{2,1,0:T(8,128)(2,1)}, bf16[4,64,1536]{2,1,0:T(8,128)(2,1)}, bf16[4,64,1536]{2,1,0:T(8,128...) custom-call(bf16[1024,2048]{1,0:T(8,128)(2,1)} %bitcast.12, ...), custom_call_target="tpu_custom_call" | custom-call | flops 4294967296 | bytes 16777216 | tf_op jit(solution)/shard_map/pallas_call | solution.py:210
  152.3 0.0 copy-start
  152.4 0.0 copy-start.2
  152.4 0.0 copy-start.3
  152.4 4.8 %all-to-all-start.1 = ((bf16[64,4,1024]{2,1,0:T(4,128)(2,1)}), bf16[64,4,1024]{2,1,0:T(4,128)(2,1)S(1)}, u32[]{:S(2)}, u32[]{:S(2)}) async-start(bf16[64,4,1024]{2,1,0:T(4,128)(2,1)} %get-tuple-element.42), calls=%async_computation.1 | async-start | bytes 1048576 | tf_op jit(solution)/shard_map/all_to_all | solution.py:229
  157.2 3.3 %collective-permute-start = (bf16[4,64,1536]{2,1,0:T(8,128)(2,1)}, bf16[4,64,1536]{2,1,0:T(8,128)(2,1)S(1)}, u32[]{:S(2)}, u32[]{:S(2)}) collective-permute-start(bf16[4,64,1536]{2,1,0:T(8,128)(2,1)} %get-tuple-element.27), channel_id=1, source_target_pairs={{0,128},{64,192},{128,0},{192,64},{256,384},{320,448},{384,256},{4... | collective-permute-start | bytes 2359304 | tf_op jit(solution)/shard_map/ppermute | solution.py:236
  160.5 4.0 %collective-permute-start.1 = (bf16[4,64,1536]{2,1,0:T(8,128)(2,1)}, bf16[4,64,1536]{2,1,0:T(8,128)(2,1)S(1)}, u32[]{:S(2)}, u32[]{:S(2)}) collective-permute-start(bf16[4,64,1536]{2,1,0:T(8,128)(2,1)} %get-tuple-element.28), channel_id=1, source_target_pairs={{0,64},{64,128},{128,192},{192,0},{256,320},{320,384},{384,448},{4... | collective-permute-start | bytes 2359304 | tf_op jit(solution)/shard_map/ppermute | solution.py:236
  164.5 1.9 collective-permute-start.2
  166.4 3.5 %collective-permute-start.6 = (bf16[4,64,1536]{2,1,0:T(8,128)(2,1)}, bf16[4,64,1536]{2,1,0:T(8,128)(2,1)S(1)}, u32[]{:S(2)}, u32[]{:S(2)}) collective-permute-start(bf16[4,64,1536]{2,1,0:T(8,128)(2,1)} %get-tuple-element.35), channel_id=1, source_target_pairs={{0,256},{64,320},{128,384},{192,448},{256,512},{320,576},{384,640}... | collective-permute-start | bytes 2359304 | tf_op jit(solution)/shard_map/ppermute | solution.py:236
  169.9 3.6 %collective-permute-start.7 = (bf16[4,64,1536]{2,1,0:T(8,128)(2,1)}, bf16[4,64,1536]{2,1,0:T(8,128)(2,1)S(1)}, u32[]{:S(2)}, u32[]{:S(2)}) collective-permute-start(bf16[4,64,1536]{2,1,0:T(8,128)(2,1)} %get-tuple-element.36), channel_id=1, source_target_pairs={{0,768},{64,832},{128,896},{192,960},{256,0},{320,64},{384,128},{4... | collective-permute-start | bytes 2359304 | tf_op jit(solution)/shard_map/ppermute | solution.py:236
  173.5 7.7 %collective-permute-done.refs_1_ = bf16[4,64,1536]{2,1,0:T(8,128)(2,1)S(1)} collective-permute-done((bf16[4,64,1536]{2,1,0:T(8,128)(2,1)}, bf16[4,64,1536]{2,1,0:T(8,128)(2,1)S(1)}, u32[]{:S(2)}, u32[]{:S(2)}) %collective-permute-start) | collective-permute-done | bytes 786464 | tf_op jit(solution)/shard_map/ppermute | solution.py:236
  181.2 5.1 %collective-permute-start.8 = (bf16[4,64,1536]{2,1,0:T(8,128)(2,1)}, bf16[4,64,1536]{2,1,0:T(8,128)(2,1)S(1)}, u32[]{:S(2)}, u32[]{:S(2)}) collective-permute-start(bf16[4,64,1536]{2,1,0:T(8,128)(2,1)} %get-tuple-element.37), channel_id=1, source_target_pairs={{0,512},{64,576},{128,640},{192,704},{256,768},{320,832},{384,896}... | collective-permute-start | bytes 2359304 | tf_op jit(solution)/shard_map/ppermute | solution.py:236
  186.3 8.5 %collective-permute-done.1.refs_2_ = bf16[4,64,1536]{2,1,0:T(8,128)(2,1)S(1)} collective-permute-done((bf16[4,64,1536]{2,1,0:T(8,128)(2,1)}, bf16[4,64,1536]{2,1,0:T(8,128)(2,1)S(1)}, u32[]{:S(2)}, u32[]{:S(2)}) %collective-permute-start.1) | collective-permute-done | bytes 786464 | tf_op jit(solution)/shard_map/ppermute | solution.py:236
  194.9 2.2 collective-permute-done.2.refs_3_
  197.0 0.0 copy-start.1
  197.0 1.1 copy-done.1
  198.2 0.4 shard_map.87
  198.5 4.9 %collective-permute-start.3 = (bf16[64,1536]{1,0:T(8,128)(2,1)S(1)}, bf16[64,1536]{1,0:T(8,128)(2,1)S(1)}, u32[]{:S(2)}, u32[]{:S(2)}) collective-permute-start(bf16[64,1536]{1,0:T(8,128)(2,1)S(1)} %get-tuple-element.31), channel_id=1, source_target_pairs={{0,768},{64,832},{128,896},{192,960},{256,0},{320,64},{384,128},{4... | collective-permute-start | bytes 589832 | tf_op jit(solution)/shard_map/ppermute | solution.py:236
  203.5 1.9 collective-permute-start.4
  205.4 0.0 collective-permute-done.6.refs_1_
  205.4 4.1 %collective-permute-start.5 = (bf16[64,1536]{1,0:T(8,128)(2,1)S(1)}, bf16[64,1536]{1,0:T(8,128)(2,1)S(1)}, u32[]{:S(2)}, u32[]{:S(2)}) collective-permute-start(bf16[64,1536]{1,0:T(8,128)(2,1)S(1)} %get-tuple-element.33), channel_id=1, source_target_pairs={{0,512},{64,576},{128,640},{192,704},{256,768},{320,832},{384,896}... | collective-permute-start | bytes 589832 | tf_op jit(solution)/shard_map/ppermute | solution.py:236
  209.5 0.0 collective-permute-done.7.refs_2_
  209.5 0.0 collective-permute-done.8.refs_3_
  209.5 0.0 copy-done
  209.5 0.4 shard_map.88
  210.0 3.5 %collective-permute-start.9 = (bf16[64,1536]{1,0:T(8,128)(2,1)S(1)}, bf16[64,1536]{1,0:T(8,128)(2,1)S(1)}, u32[]{:S(2)}, u32[]{:S(2)}) collective-permute-start(bf16[64,1536]{1,0:T(8,128)(2,1)S(1)} %get-tuple-element.39), channel_id=1, source_target_pairs={{0,128},{64,192},{128,0},{192,64},{256,384},{320,448},{384,256},{4... | collective-permute-start | bytes 589832 | tf_op jit(solution)/shard_map/ppermute | solution.py:236
  213.4 3.8 %collective-permute-start.10 = (bf16[64,1536]{1,0:T(8,128)(2,1)S(1)}, bf16[64,1536]{1,0:T(8,128)(2,1)S(1)}, u32[]{:S(2)}, u32[]{:S(2)}) collective-permute-start(bf16[64,1536]{1,0:T(8,128)(2,1)S(1)} %get-tuple-element.40), channel_id=1, source_target_pairs={{0,64},{64,128},{128,192},{192,0},{256,320},{320,384},{384,448},{4... | collective-permute-start | bytes 589832 | tf_op jit(solution)/shard_map/ppermute | solution.py:236
  217.3 0.0 collective-permute-done.3.refs_1_
  217.3 2.0 collective-permute-start.11
  219.3 0.0 collective-permute-done.4.refs_2_
  219.3 0.0 collective-permute-done.5.refs_3_
  219.3 0.0 collective-permute-done.9.refs_5_
  219.3 3.6 %collective-permute-done.10.refs_6_ = bf16[64,1536]{1,0:T(8,128)(2,1)S(1)} collective-permute-done((bf16[64,1536]{1,0:T(8,128)(2,1)S(1)}, bf16[64,1536]{1,0:T(8,128)(2,1)S(1)}, u32[]{:S(2)}, u32[]{:S(2)}) %collective-permute-start.10) | collective-permute-done | bytes 196640 | tf_op jit(solution)/shard_map/ppermute | solution.py:236
  223.0 3.1 %collective-permute-done.11.refs_7_ = bf16[64,1536]{1,0:T(8,128)(2,1)S(1)} collective-permute-done((bf16[64,1536]{1,0:T(8,128)(2,1)S(1)}, bf16[64,1536]{1,0:T(8,128)(2,1)S(1)}, u32[]{:S(2)}, u32[]{:S(2)}) %collective-permute-start.11) | collective-permute-done | bytes 196640 | tf_op jit(solution)/shard_map/ppermute | solution.py:236
  226.1 0.0 all-to-all-done.1.refs_8_
  226.1 0.0 copy-done.2
  226.1 0.0 copy-done.3
  226.1 1.2 shard_map.89
Async XLA Ops:
  152.3 57.2 %copy-start = (bf16[4,64,1536]{2,1,0:T(8,128)(2,1)S(1)}, bf16[4,64,1536]{2,1,0:T(8,128)(2,1)}, u32[]{:S(2)}) copy-start(bf16[4,64,1536]{2,1,0:T(8,128)(2,1)} %get-tuple-element.34.refs_0_) | copy-start | bytes 2359300
  152.4 73.7 %copy-start.2 = (f32[128,1]{0,1:T(1,128)S(1)}, f32[128,1]{0,1:T(1,128)}, u32[]{:S(2)}) copy-start(f32[128,1]{0,1:T(1,128)} %param.9) | copy-start | bytes 1540
  152.4 73.7 %copy-start.3 = (s32[1,128]{1,0:T(1,128)S(1)}, s32[1,128]{1,0:T(1,128)}, u32[]{:S(2)}) copy-start(s32[1,128]{1,0:T(1,128)} %get-tuple-element.43.refs_9_) | copy-start | bytes 1540
  152.4 73.7 %all-to-all-start.1 = ((bf16[64,4,1024]{2,1,0:T(4,128)(2,1)}), bf16[64,4,1024]{2,1,0:T(4,128)(2,1)S(1)}, u32[]{:S(2)}, u32[]{:S(2)}) async-start(bf16[64,4,1024]{2,1,0:T(4,128)(2,1)} %get-tuple-element.42), calls=%async_computation.1 | async-start | bytes 1048576 | tf_op jit(solution)/shard_map/all_to_all | solution.py:229
  157.2 24.1 %collective-permute-start = (bf16[4,64,1536]{2,1,0:T(8,128)(2,1)}, bf16[4,64,1536]{2,1,0:T(8,128)(2,1)S(1)}, u32[]{:S(2)}, u32[]{:S(2)}) collective-permute-start(bf16[4,64,1536]{2,1,0:T(8,128)(2,1)} %get-tuple-element.27), channel_id=1, source_target_pairs={{0,128},{64,192},{128,0},{192,64},{256,384},{320,448},{384,256},{4... | collective-permute-start | bytes 2359304 | tf_op jit(solution)/shard_map/ppermute | solution.py:236
  160.5 34.4 %collective-permute-start.1 = (bf16[4,64,1536]{2,1,0:T(8,128)(2,1)}, bf16[4,64,1536]{2,1,0:T(8,128)(2,1)S(1)}, u32[]{:S(2)}, u32[]{:S(2)}) collective-permute-start(bf16[4,64,1536]{2,1,0:T(8,128)(2,1)} %get-tuple-element.28), channel_id=1, source_target_pairs={{0,64},{64,128},{128,192},{192,0},{256,320},{320,384},{384,448},{4... | collective-permute-start | bytes 2359304 | tf_op jit(solution)/shard_map/ppermute | solution.py:236
  164.5 32.5 %collective-permute-start.2 = (bf16[4,64,1536]{2,1,0:T(8,128)(2,1)}, bf16[4,64,1536]{2,1,0:T(8,128)(2,1)S(1)}, u32[]{:S(2)}, u32[]{:S(2)}) collective-permute-start(bf16[4,64,1536]{2,1,0:T(8,128)(2,1)} %get-tuple-element.29), channel_id=1, source_target_pairs={{0,192},{64,0},{128,64},{192,128},{256,448},{320,256},{384,320},{4... | collective-permute-start | bytes 2359304 | tf_op jit(solution)/shard_map/ppermute | solution.py:236
  166.4 39.0 %collective-permute-start.6 = (bf16[4,64,1536]{2,1,0:T(8,128)(2,1)}, bf16[4,64,1536]{2,1,0:T(8,128)(2,1)S(1)}, u32[]{:S(2)}, u32[]{:S(2)}) collective-permute-start(bf16[4,64,1536]{2,1,0:T(8,128)(2,1)} %get-tuple-element.35), channel_id=1, source_target_pairs={{0,256},{64,320},{128,384},{192,448},{256,512},{320,576},{384,640}... | collective-permute-start | bytes 2359304 | tf_op jit(solution)/shard_map/ppermute | solution.py:236
  169.9 39.6 %collective-permute-start.7 = (bf16[4,64,1536]{2,1,0:T(8,128)(2,1)}, bf16[4,64,1536]{2,1,0:T(8,128)(2,1)S(1)}, u32[]{:S(2)}, u32[]{:S(2)}) collective-permute-start(bf16[4,64,1536]{2,1,0:T(8,128)(2,1)} %get-tuple-element.36), channel_id=1, source_target_pairs={{0,768},{64,832},{128,896},{192,960},{256,0},{320,64},{384,128},{4... | collective-permute-start | bytes 2359304 | tf_op jit(solution)/shard_map/ppermute | solution.py:236
  181.2 28.3 %collective-permute-start.8 = (bf16[4,64,1536]{2,1,0:T(8,128)(2,1)}, bf16[4,64,1536]{2,1,0:T(8,128)(2,1)S(1)}, u32[]{:S(2)}, u32[]{:S(2)}) collective-permute-start(bf16[4,64,1536]{2,1,0:T(8,128)(2,1)} %get-tuple-element.37), channel_id=1, source_target_pairs={{0,512},{64,576},{128,640},{192,704},{256,768},{320,832},{384,896}... | collective-permute-start | bytes 2359304 | tf_op jit(solution)/shard_map/ppermute | solution.py:236
  197.0 1.1 copy-start.1
  198.5 18.8 %collective-permute-start.3 = (bf16[64,1536]{1,0:T(8,128)(2,1)S(1)}, bf16[64,1536]{1,0:T(8,128)(2,1)S(1)}, u32[]{:S(2)}, u32[]{:S(2)}) collective-permute-start(bf16[64,1536]{1,0:T(8,128)(2,1)S(1)} %get-tuple-element.31), channel_id=1, source_target_pairs={{0,768},{64,832},{128,896},{192,960},{256,0},{320,64},{384,128},{4... | collective-permute-start | bytes 589832 | tf_op jit(solution)/shard_map/ppermute | solution.py:236
  203.5 15.8 %collective-permute-start.4 = (bf16[64,1536]{1,0:T(8,128)(2,1)S(1)}, bf16[64,1536]{1,0:T(8,128)(2,1)S(1)}, u32[]{:S(2)}, u32[]{:S(2)}) collective-permute-start(bf16[64,1536]{1,0:T(8,128)(2,1)S(1)} %get-tuple-element.32), channel_id=1, source_target_pairs={{0,256},{64,320},{128,384},{192,448},{256,512},{320,576},{384,640}... | collective-permute-start | bytes 589832 | tf_op jit(solution)/shard_map/ppermute | solution.py:236
  205.4 13.9 %collective-permute-start.5 = (bf16[64,1536]{1,0:T(8,128)(2,1)S(1)}, bf16[64,1536]{1,0:T(8,128)(2,1)S(1)}, u32[]{:S(2)}, u32[]{:S(2)}) collective-permute-start(bf16[64,1536]{1,0:T(8,128)(2,1)S(1)} %get-tuple-element.33), channel_id=1, source_target_pairs={{0,512},{64,576},{128,640},{192,704},{256,768},{320,832},{384,896}... | collective-permute-start | bytes 589832 | tf_op jit(solution)/shard_map/ppermute | solution.py:236
  210.0 9.4 %collective-permute-start.9 = (bf16[64,1536]{1,0:T(8,128)(2,1)S(1)}, bf16[64,1536]{1,0:T(8,128)(2,1)S(1)}, u32[]{:S(2)}, u32[]{:S(2)}) collective-permute-start(bf16[64,1536]{1,0:T(8,128)(2,1)S(1)} %get-tuple-element.39), channel_id=1, source_target_pairs={{0,128},{64,192},{128,0},{192,64},{256,384},{320,448},{384,256},{4... | collective-permute-start | bytes 589832 | tf_op jit(solution)/shard_map/ppermute | solution.py:236
  213.4 9.5 %collective-permute-start.10 = (bf16[64,1536]{1,0:T(8,128)(2,1)S(1)}, bf16[64,1536]{1,0:T(8,128)(2,1)S(1)}, u32[]{:S(2)}, u32[]{:S(2)}) collective-permute-start(bf16[64,1536]{1,0:T(8,128)(2,1)S(1)} %get-tuple-element.40), channel_id=1, source_target_pairs={{0,64},{64,128},{128,192},{192,0},{256,320},{320,384},{384,448},{4... | collective-permute-start | bytes 589832 | tf_op jit(solution)/shard_map/ppermute | solution.py:236
  217.3 8.8 %collective-permute-start.11 = (bf16[64,1536]{1,0:T(8,128)(2,1)S(1)}, bf16[64,1536]{1,0:T(8,128)(2,1)S(1)}, u32[]{:S(2)}, u32[]{:S(2)}) collective-permute-start(bf16[64,1536]{1,0:T(8,128)(2,1)S(1)} %get-tuple-element.41), channel_id=1, source_target_pairs={{0,192},{64,0},{128,64},{192,128},{256,448},{320,256},{384,320},{4... | collective-permute-start | bytes 589832 | tf_op jit(solution)/shard_map/ppermute | solution.py:236
